TPU v7x, 32 devices: a whole 2x2x4 slice. The times are simulated.
32 devices in a mesh: ctx: 8 (over y, x, core), grp: 4 (over z).
Axes of the slice: x: 2, y: 2, z: 4, core: 2. Of those that a mesh axis runs over, the one named last changes fastest.
Arguments:
- residual: bfloat16 [4, 1024, 2880], P('grp', 'ctx'), may hold values from -3 to 3
- queries: bfloat16 [4, 1024, 2048], P('grp', 'ctx'), may hold values from -8 to 8
- stretch_kv: bfloat16 [4, 1024, 1024], P('grp', 'ctx'), may hold values from -8 to 8
- cache_kv: bfloat16 [4, 2048, 1024], P('grp', 'ctx'), may hold values from -6 to 6
- doc_lengths: int32 [4, 8], P('grp'), may hold values from 1 to 1536, 3072 in all within a row
- sinks: float32 [32], replicated, may hold values from 2 to 6
- out_proj: bfloat16 [2048, 2880], P('ctx'), may hold values from -0.75 to 0.75
- norm_gain: float32 [2880], replicated, may hold values from 0.1 to 1.9
- router: bfloat16 [2880, 16], replicated, may hold values from -0.109375 to 0.109375
- expert_ids: int32 [4, 1024, 4], P('grp', 'ctx'), may hold values from 0 to 15, all different within a row; in each aligned block of 128 rows (0 to 127, 128 to 255, ..., all dimensions but the last counted through in order) at most 40 rows name the same one
- expert_in: bfloat16 [32, 2880, 1536], P(('ctx', 'grp')), may hold values from -0.109375 to 0.109375
- expert_out: bfloat16 [32, 768, 2880], P(('ctx', 'grp')), may hold values from -0.15625 to 0.15625
Outputs:
- resid_mid: bfloat16 [4, 1024, 2880], P('grp', 'ctx')
- layer_out: bfloat16 [4, 1024, 2880], P('grp', 'ctx')
Inputs may be any that keep to these rules, and one draw needn't show every extreme that they name: `expert_ids`: in the rows of one device (aligned blocks of 128 tokens, sequence after sequence), each expert is named by at most 40 rows, and in some blocks one expert by exactly 40; a token's 4 experts differ. `doc_lengths`: A sequence's 8 lengths sum to 3072; the longest is exactly 1536.
All inputs are finite; a program needn't handle non-finite values.
Results may differ from a plain program's by a relative error of at most 0.015.
Values may be sent and summed in bfloat16 or wider, within the bound.
A program may use at most 128 MiB of HBM per device.

v0:
```python
import math

import jax
import jax.numpy as jnp
from jax import lax
from jax.sharding import PartitionSpec as P

HEADS = 32
KVH = 8
HD = 64


def doc_index(positions, lengths):
    ends = jnp.cumsum(lengths)
    return jnp.sum((positions[:, None] >= ends[None, :]).astype(jnp.int32), axis=1)


def gated_act(pre, half_width):
    gate = pre[:, :half_width]
    upper = pre[:, half_width:]
    return ((upper + 1.0) * gate * jax.nn.sigmoid(1.702 * gate)).astype(jnp.bfloat16)


def body(
    residual,
    queries,
    stretch_kv,
    cache_kv,
    doc_lengths,
    sinks,
    out_proj,
    norm_gain,
    router,
    expert_ids,
    expert_in,
    expert_out,
):
    tokens = residual.shape[1]
    width = residual.shape[2]
    cache_rows = cache_kv.shape[1]
    kv_cols = stretch_kv.shape[2] // 2
    groups = HEADS // KVH
    ctx_count = lax.axis_size("ctx")
    ctx_here = lax.axis_index("ctx")
    stretch_base = cache_rows * ctx_count
    span = cache_rows + tokens
    query_pos = stretch_base + ctx_here * tokens + jnp.arange(tokens, dtype=jnp.int32)
    lengths = doc_lengths[0]
    query_doc = doc_index(query_pos, lengths)
    query_heads = queries[0].reshape(tokens, KVH, groups, HD)
    sink_grid = sinks.reshape(KVH, groups)
    local_kv = jnp.concatenate([cache_kv[0], stretch_kv[0]], axis=0)
    scale = 1.0 / math.sqrt(HD)

    def key_block(carry, keys_values, first):
        count = keys_values.shape[0]
        rows = first + jnp.arange(count, dtype=jnp.int32)
        source = rows // span
        offset = rows % span
        key_pos = jnp.where(
            offset < cache_rows,
            source * cache_rows + offset,
            stretch_base + source * tokens + offset - cache_rows,
        )
        key_doc = doc_index(key_pos, lengths)
        allowed = (key_pos[None, :] <= query_pos[:, None]) & (
            key_doc[None, :] == query_doc[:, None]
        )
        keys = keys_values[:, :kv_cols].reshape(count, KVH, HD)
        values = keys_values[:, kv_cols:].reshape(count, KVH, HD)
        top, total, numer = carry
        scores = (
            jnp.einsum("qkgd,skd->kgqs", query_heads, keys, preferred_element_type=jnp.float32)
            * scale
        )
        masked = jnp.where(allowed[None, None], scores, -jnp.inf)
        new_top = jnp.maximum(top, jnp.max(masked, axis=-1))
        weights = jnp.where(allowed[None, None], jnp.exp(scores - new_top[..., None]), 0.0)
        shrink = jnp.exp(top - new_top)
        total = total * shrink + jnp.sum(weights, axis=-1)
        numer = numer * shrink[..., None] + jnp.einsum(
            "kgqs,skd->kgqd",
            weights.astype(jnp.bfloat16),
            values,
            preferred_element_type=jnp.float32,
        )
        return (new_top, total, numer)

    start_top = jnp.broadcast_to(sink_grid[:, :, None], (KVH, groups, tokens))
    start_total = jnp.zeros((KVH, groups, tokens), jnp.float32)
    start_numer = jnp.zeros((KVH, groups, tokens, HD), jnp.float32)
    piece = lax.all_gather(local_kv, "ctx", axis=0, tiled=True)
    count = piece.shape[0]
    step_rows = math.gcd(count, 1024)

    def advance(index, state):
        first = index * step_rows
        part = lax.dynamic_slice_in_dim(piece, first, step_rows, 0)
        return key_block(state, part, first)

    top, total, numer = lax.fori_loop(
        0, count // step_rows, advance, (start_top, start_total, start_numer)
    )
    denom = total + jnp.exp(sink_grid[:, :, None] - top)
    attended = (
        jnp.transpose(numer / denom[..., None], (2, 0, 1, 3))
        .reshape(tokens, HEADS * HD)
        .astype(jnp.bfloat16)
    )
    projected = jnp.dot(
        attended,
        lax.all_gather(out_proj, "ctx", axis=0, tiled=True),
        preferred_element_type=jnp.float32,
    )
    mid = (residual[0].astype(jnp.float32) + projected).astype(jnp.bfloat16)
    mid_float = mid.astype(jnp.float32)
    normed = (
        mid_float
        * lax.rsqrt(jnp.mean(mid_float * mid_float, axis=-1, keepdims=True) + 1e-05)
        * norm_gain
    ).astype(jnp.bfloat16)
    logits = jnp.dot(normed, router, preferred_element_type=jnp.float32)
    experts = router.shape[1]
    chosen_ids = expert_ids[0]
    topk = chosen_ids.shape[1]
    picks = chosen_ids[:, :, None] == jnp.arange(experts, dtype=jnp.int32)[None, None, :]
    chosen = jnp.sum(jnp.where(picks, logits[:, None, :], 0.0), axis=-1)
    raised = jnp.exp(chosen)
    route_weights = raised / jnp.sum(raised, axis=-1, keepdims=True)
    capacity = 2 * ((5 * tokens * topk + 8 * experts - 1) // (8 * experts))
    flat_ids = chosen_ids.reshape(-1)
    pairs = flat_ids.shape[0]
    onehot = (flat_ids[:, None] == jnp.arange(experts, dtype=jnp.int32)[None, :]).astype(jnp.int32)
    slots = jnp.sum(onehot * (jnp.cumsum(onehot, axis=0) - 1), axis=1)
    dest = flat_ids * capacity + slots
    source_rows = jnp.arange(pairs, dtype=jnp.int32) // topk
    packed = jnp.zeros((experts * capacity, width), jnp.bfloat16).at[dest].set(normed[source_rows])
    packed = packed.reshape(experts, capacity, width)
    in_weights = expert_in[0]
    out_weights = expert_out[0]
    half_width = out_weights.shape[0]
    doubled = jnp.broadcast_to(packed[:, None], (experts, 2, capacity, width)).reshape(
        2 * experts, capacity, width
    )
    received = lax.all_to_all(doubled, ("ctx", "grp"), split_axis=0, concat_axis=0, tiled=True)
    flat_rows = received.reshape(-1, width)
    pre = jnp.dot(flat_rows, in_weights, preferred_element_type=jnp.float32)
    hidden = gated_act(pre, half_width)
    partial_out = jnp.dot(hidden, out_weights, preferred_element_type=jnp.float32).astype(
        jnp.bfloat16
    )
    partial_out = partial_out.reshape(received.shape)
    returned = lax.all_to_all(partial_out, ("ctx", "grp"), split_axis=0, concat_axis=0, tiled=True)
    pair_total = jnp.sum(returned.reshape(experts, 2, capacity, width).astype(jnp.float32), axis=1)
    expert_rows = pair_total.astype(jnp.bfloat16).reshape(experts * capacity, width)
    gathered = expert_rows[dest].astype(jnp.float32) * route_weights.reshape(-1)[:, None]
    mixture = jnp.sum(gathered.reshape(tokens, topk, width), axis=1)
    final = (mid_float + mixture).astype(jnp.bfloat16)
    return (mid[None], final[None])


def solution(mesh):
    return jax.shard_map(
        body,
        mesh=mesh,
        in_specs=(
            P("grp", "ctx", None),
            P("grp", "ctx", None),
            P("grp", "ctx", None),
            P("grp", "ctx", None),
            P("grp", None),
            P(),
            P("ctx", None),
            P(),
            P(),
            P("grp", "ctx", None),
            P(("ctx", "grp"), None, None),
            P(("ctx", "grp"), None, None),
        ),
        out_specs=(P("grp", "ctx", None), P("grp", "ctx", None)),
        check_vma=False,
    )
```

profile of v0, /device:TPU:0, one launch (start us, length us, event | category | flops | bytes accessed | tf_op | source)
XLA Modules:
  0.0 578.9 jit_solution(18386660075242664453)
XLA Ops:
  7.3 1.3 copy.47
  8.6 1.1 copy.48
  9.7 1.0 pad_maximum_fusion
  10.8 0.7 all-gather.5.cloned.1.call-update
  11.9 0.2 broadcast_in_dim.135
  12.1 0.2 reduce-window.19
  12.3 0.3 copy.49
  12.6 1.2 reduce-window.20
  13.7 0.2 slice_reduce_fusion
  14.0 0.1 copy.50
  14.5 45.8 %all-gather.3.cloned.1.call-done = bf16[3072,1024]{0,1:T(8,128)(2,1)} async-done(((bf16[384,1024]{0,1:T(8,128)(2,1)}), bf16[3072,1024]{0,1:T(8,128)(2,1)}) %all-gather.3.cloned.1.call-update) | async-done | bytes 6291472 | tf_op jit(solution)/shard_map/all_gather | solution.py:92
  60.4 81.1 %while.20 = (s32[]{:T(128)}, f32[8,4,128]{2,1,0:T(4,128)S(1)}, f32[8,4,128]{2,1,0:T(4,128)S(1)}, f32[8,4,128,64]{2,3,1,0:T(8,128)S(1)}, s32[1,8]{1,0:T(1,128)S(1...) while((s32[]{:T(128)}, f32[8,4,128]{2,1,0:T(4,128)S(1)}, ...), condition=%wide.region_7.8_spmd.clone, body=%wide.region_3.7_spmd.clone.sunk | while | flops 1121116288 | bytes 60053240 | solution.py:101
  60.4 1.7 fusion.68
  62.2 0.3 compare_and_fusion.2
  62.5 7.4 %fusion.69 = (f32[8,4,128]{2,1,0:T(4,128)S(1)}, f32[8,1024,128,4]{2,1,3,0:T(8,128)}) fusion(pred[128,1024]{0,1:T(8,128)(4,1)S(1)} %compare_and_fusion.2, bf16[1024,8,64,1]{0,2,3,1:T(8,128)(2,1)S(1)} %bitcast.100, bf16[128,8,4,64]{0,3,2,1:T(8,128)(2,1)S(1)} %get-tuple-element.394), kind=kOutput, calls=%fused_computation.6.clone.1 | convolution fusion | flops 549449728 | bytes 18497536 | tf_op jit(solution)/shard_map/while/body/eval_jaxpr/qkgd,skd->kgqs/dot_general | solution.py:73
  70.0 9.9 %fusion.70 = f32[8,4,128]{2,1,0:T(4,128)S(1)} fusion(f32[8,1024,128,4]{2,1,3,0:T(8,128)} %get-tuple-element.355, f32[8,4,128]{2,1,0:T(4,128)S(1)} %max.12, pred[128,1024]{0,1:T(8,128)(4,1)S(1)} %compare_and_fusion.2), kind=kLoop, calls=%fused_computation.10.clone.1 | loop fusion | flops 16773120 | bytes 16941056 | tf_op jit(solution)/shard_map/while/body/eval_jaxpr/reduce_sum | solution.py:80
  80.0 7.4 %fusion.72 = f32[8,4,128,64]{2,3,1,0:T(8,128)S(1)} fusion(bf16[1024,8,64,1]{0,2,3,1:T(8,128)(2,1)S(1)} %bitcast.104, f32[8,1024,128,4]{2,1,3,0:T(8,128)} %get-tuple-element.355, f32[8,4,128]{2,1,0:T(4,128)S(1)} %max.12, pred[128,1024]{0,1:T(8,128)(4,1)S(1)} %compare_and_fusion.2, f32[8,4,128,64]{2,3,1,0:T(8,128)S(1)} %get-tuple-element.376, ...), kind=kOutput, calls=%fused_computation.13.clone.1 | convolution fusion | flops 554434560 | bytes 20086784 | tf_op jit(solution)/shard_map/while/body/eval_jaxpr/kgqs,skd->kgqd/dot_general | solution.py:81
  87.5 1.7 fusion.68
  89.3 0.3 compare_and_fusion.2
  89.6 8.0 %fusion.69 = (f32[8,4,128]{2,1,0:T(4,128)S(1)}, f32[8,1024,128,4]{2,1,3,0:T(8,128)}) fusion(pred[128,1024]{0,1:T(8,128)(4,1)S(1)} %compare_and_fusion.2, bf16[1024,8,64,1]{0,2,3,1:T(8,128)(2,1)S(1)} %bitcast.100, bf16[128,8,4,64]{0,3,2,1:T(8,128)(2,1)S(1)} %get-tuple-element.394), kind=kOutput, calls=%fused_computation.6.clone.1 | convolution fusion | flops 549449728 | bytes 18497536 | tf_op jit(solution)/shard_map/while/body/eval_jaxpr/qkgd,skd->kgqs/dot_general | solution.py:73
  97.7 9.8 %fusion.70 = f32[8,4,128]{2,1,0:T(4,128)S(1)} fusion(f32[8,1024,128,4]{2,1,3,0:T(8,128)} %get-tuple-element.355, f32[8,4,128]{2,1,0:T(4,128)S(1)} %max.12, pred[128,1024]{0,1:T(8,128)(4,1)S(1)} %compare_and_fusion.2), kind=kLoop, calls=%fused_computation.10.clone.1 | loop fusion | flops 16773120 | bytes 16941056 | tf_op jit(solution)/shard_map/while/body/eval_jaxpr/reduce_sum | solution.py:80
  107.5 7.4 %fusion.72 = f32[8,4,128,64]{2,3,1,0:T(8,128)S(1)} fusion(bf16[1024,8,64,1]{0,2,3,1:T(8,128)(2,1)S(1)} %bitcast.104, f32[8,1024,128,4]{2,1,3,0:T(8,128)} %get-tuple-element.355, f32[8,4,128]{2,1,0:T(4,128)S(1)} %max.12, pred[128,1024]{0,1:T(8,128)(4,1)S(1)} %compare_and_fusion.2, f32[8,4,128,64]{2,3,1,0:T(8,128)S(1)} %get-tuple-element.376, ...), kind=kOutput, calls=%fused_computation.13.clone.1 | convolution fusion | flops 554434560 | bytes 20086784 | tf_op jit(solution)/shard_map/while/body/eval_jaxpr/kgqs,skd->kgqd/dot_general | solution.py:81
  115.0 1.7 fusion.68
  116.9 0.3 compare_and_fusion.2
  117.2 7.0 %fusion.69 = (f32[8,4,128]{2,1,0:T(4,128)S(1)}, f32[8,1024,128,4]{2,1,3,0:T(8,128)}) fusion(pred[128,1024]{0,1:T(8,128)(4,1)S(1)} %compare_and_fusion.2, bf16[1024,8,64,1]{0,2,3,1:T(8,128)(2,1)S(1)} %bitcast.100, bf16[128,8,4,64]{0,3,2,1:T(8,128)(2,1)S(1)} %get-tuple-element.394), kind=kOutput, calls=%fused_computation.6.clone.1 | convolution fusion | flops 549449728 | bytes 18497536 | tf_op jit(solution)/shard_map/while/body/eval_jaxpr/qkgd,skd->kgqs/dot_general | solution.py:73
  124.3 9.3 %fusion.70 = f32[8,4,128]{2,1,0:T(4,128)S(1)} fusion(f32[8,1024,128,4]{2,1,3,0:T(8,128)} %get-tuple-element.355, f32[8,4,128]{2,1,0:T(4,128)S(1)} %max.12, pred[128,1024]{0,1:T(8,128)(4,1)S(1)} %compare_and_fusion.2), kind=kLoop, calls=%fused_computation.10.clone.1 | loop fusion | flops 16773120 | bytes 16941056 | tf_op jit(solution)/shard_map/while/body/eval_jaxpr/reduce_sum | solution.py:80
  133.6 7.4 %fusion.72 = f32[8,4,128,64]{2,3,1,0:T(8,128)S(1)} fusion(bf16[1024,8,64,1]{0,2,3,1:T(8,128)(2,1)S(1)} %bitcast.104, f32[8,1024,128,4]{2,1,3,0:T(8,128)} %get-tuple-element.355, f32[8,4,128]{2,1,0:T(4,128)S(1)} %max.12, pred[128,1024]{0,1:T(8,128)(4,1)S(1)} %compare_and_fusion.2, f32[8,4,128,64]{2,3,1,0:T(8,128)S(1)} %get-tuple-element.376, ...), kind=kOutput, calls=%fused_computation.13.clone.1 | convolution fusion | flops 554434560 | bytes 20086784 | tf_op jit(solution)/shard_map/while/body/eval_jaxpr/kgqs,skd->kgqd/dot_general | solution.py:81
  141.6 0.1 divide_convert_fusion
  141.8 7.7 %fusion.35 = (f32[128]{0:T(128)S(1)}, bf16[128,2880]{0,1:T(8,128)(2,1)S(1)}) fusion(bf16[2048,2880]{0,1:T(8,128)(2,1)} %all-gather.5.cloned.1.call-done, bf16[128,2048]{0,1:T(8,128)(2,1)S(1)} %bitcast.110, bf16[1,128,2880]{1,2,0:T(8,128)(2,1)} %param.14), kind=kOutput, calls=%fused_computation.55 | convolution fusion | flops 1512161152 | bytes 13795840 | tf_op jit(solution)/shard_map/dot_general | solution.py:110
  149.5 0.8 copy-done.1
  150.4 0.4 fusion.37
  150.8 0.4 copy.54
  151.2 16.3 %scatter_custom_fusion = bf16[640,2880]{1,0:T(8,128)(2,1)} fusion(s32[512]{0:T(512)S(1)} %bitcast.113, bf16[128,2880]{1,0:T(8,128)(2,1)S(1)} %copy.54, s32[1024]{0:T(1024)S(1)} %pad_clamp_fusion.1, bf16[]{:T(256)} %constant.176.clone.1), kind=kCustom, calls=%fused_computation.47 | custom fusion | bytes 3686402 | tf_op jit(solution)/shard_map/scatter | solution.py:137
  167.5 2.6 broadcast_in_dim.139
  170.1 171.0 %all_to_all.10 = bf16[32,40,2880]{2,1,0:T(8,128)(2,1)S(1)} all-to-all(bf16[32,40,2880]{2,1,0:T(8,128)(2,1)S(1)} %bitcast.103), channel_id=1, replica_groups=mesh['ctx'=8,'grp'=4] {'ctx','grp'}, dimensions={0} | all-to-all | bytes 14745600 | tf_op jit(solution)/shard_map/all_to_all | solution.py:145
  341.0 15.3 %fusion.22 = f32[1280,1536]{1,0:T(8,128)S(1)} fusion(bf16[1280,2880]{1,0:T(8,128)(2,1)S(1)} %bitcast.106, bf16[1,2880,1536]{2,1,0:T(8,128)(2,1)} %param.24), kind=kOutput, calls=%fused_computation.36 | convolution fusion | flops 11324620800 | bytes 24084480 | tf_op jit(solution)/shard_map/dot_general | solution.py:147
  356.4 8.3 %convolution_convert_fusion = bf16[1280,2880]{0,1:T(8,128)(2,1)} fusion(bf16[1,768,2880]{1,2,0:T(8,128)(2,1)S(1)} %bitcast.118, f32[1280,1536]{1,0:T(8,128)S(1)} %fusion.22), kind=kOutput, calls=%fused_computation.35 | convolution fusion | flops 5673861120 | bytes 19660800 | tf_op jit(solution)/shard_map/dot_general | solution.py:149
  364.7 10.4 %copy.55 = bf16[1280,2880]{1,0:T(8,128)(2,1)} copy(bf16[1280,2880]{0,1:T(8,128)(2,1)} %convolution_convert_fusion) | data formatting | bytes 14745600 | tf_op jit(solution)/shard_map/convert_element_type | solution.py:149
  375.2 4.0 all-to-all-start.1
  379.2 0.2 fusion.46
  379.5 0.1 copy.56
  379.6 163.0 %all-to-all-done.1 = bf16[32,40,2880]{2,1,0:T(8,128)(2,1)} async-done(((bf16[32,40,2880]{2,1,0:T(8,128)(2,1)}), bf16[32,40,2880]{2,1,0:T(8,128)(2,1)}, u32[]{:S(2)}, u32[]{:S(2)}) %all-to-all-start.1) | async-done | bytes 7372832 | tf_op jit(solution)/shard_map/all_to_all | solution.py:153
  542.6 7.4 %bitcast_reduce_fusion = bf16[16,40,2880]{2,1,0:T(8,128)(2,1)} fusion(bf16[32,40,2880]{2,1,0:T(8,128)(2,1)} %all-to-all-done.1), kind=kLoop, calls=%fused_computation.38 | loop fusion | flops 1843200 | bytes 11059200 | tf_op jit(solution)/shard_map/reduce_sum | solution.py:154
  549.9 8.4 %gather_fusion = bf16[512,2880]{1,0:T(8,128)(2,1)S(1)} fusion(bf16[640,2880]{1,0:T(8,128)(2,1)} %bitcast.99, s32[1024]{0:T(1024)S(1)} %pad_clamp_fusion), kind=kCustom, calls=%fused_computation.1 | custom fusion | bytes 5900288 | tf_op jit(solution)/shard_map/gather | solution.py:156
  558.3 3.6 reshape.325
  561.9 7.1 %multiply_reduce_fusion = f32[128,2880]{1,0:T(8,128)S(1)} fusion(f32[128,4,2880]{2,1,0:T(4,128)} %reshape.325, f32[128,4]{1,0:T(8,128)S(1)} %copy.56), kind=kLoop, calls=%fused_computation.39 | loop fusion | flops 2580480 | bytes 7374848 | tf_op jit(solution)/shard_map/reduce_sum | solution.py:157
  569.0 0.4 copy.57
  569.5 2.2 fusion.39
  (66 shorter events, 1.6 us)
Async XLA Ops:
  7.2 372.0 %copy-start = (bf16[2880,16]{0,1:T(8,128)(2,1)S(1)}, bf16[2880,16]{0,1:T(8,128)(2,1)}, u32[]{:S(2)}) copy-start(bf16[2880,16]{0,1:T(8,128)(2,1)} %param.22) | copy-start | bytes 276484
  7.2 4.3 copy-start.3
  7.2 4.6 copy-start.6
  7.2 4.7 copy-start.7
  7.2 5.1 copy-start.2
  7.2 53.1 %all-gather.3.cloned.1.call-start = ((), (), s32[]{:S(2)}) async-start(), calls=%async_computation.2 | async-start | bytes 7077888 | tf_op jit(solution)/shard_map/all_gather | solution.py:92
  10.7 131.0 %all-gather.5.cloned.1.call-start = ((), (), s32[]{:S(2)}) async-start(), calls=%async_computation.3 | async-start | bytes 13271040 | tf_op jit(solution)/shard_map/all_gather | solution.py:112
  141.8 8.6 %copy-start.5 = (f32[2880]{0:T(1024)S(1)}, f32[2880]{0:T(1024)}, u32[]{:S(2)}) copy-start(f32[2880]{0:T(1024)} %param.21) | copy-start | bytes 34564
  149.5 0.9 copy-start.1
  170.1 186.3 %slice-start = ((s8[4423680]{0:T(1024)(128)(4,1)}), s8[4194304]{0:T(1024)(128)(4,1)S(1)}, s32[]{:S(2)}) async-start(s8[4423680]{0:T(1024)(128)(4,1)} %bitcast.117), calls=%async_computation.4 | async-start | bytes 8388608
  341.0 15.3 %slice-start.1 = ((s8[4423680]{0:T(1024)(128)(4,1)}), s8[229376]{0:T(1024)(128)(4,1)S(1)}, s32[]{:S(2)}) async-start(s8[4423680]{0:T(1024)(128)(4,1)} %bitcast.117), calls=%async_computation.5 | async-start | bytes 458752
  375.1 4.3 copy-start.4
  375.2 167.4 %all-to-all-start.1 = ((bf16[32,40,2880]{2,1,0:T(8,128)(2,1)}), bf16[32,40,2880]{2,1,0:T(8,128)(2,1)}, u32[]{:S(2)}, u32[]{:S(2)}) async-start(bf16[32,40,2880]{2,1,0:T(8,128)(2,1)} %bitcast.102), calls=%async_computation.1 | async-start | bytes 15073280 | tf_op jit(solution)/shard_map/all_to_all | solution.py:153
Sparse Core Ops, SparseCore 0:
  10.8 49.4 all-gather.2
  62.2 71.0 all-gather.4
where the time goes:
time: 589 us; the launch traced here: 579 us
  waiting for transfers between devices  210 us (36%)
  blocking collectives  171 us (29%)
  matrix products  76.5 us (13%)
  local copies, waits for them, and re-layouts  51.9 us (9%)
  other arithmetic  50.5 us (9%)
  between operations  14.8 us (3%)
    all_to_all x1, blocking collectives, body(): lax.all_to_all(doubled, ('ctx', 'grp'), split_axis=0, concat_axis=0, tile...  171 us
    all_to_all x1, waiting for transfers between devices, body(): lax.all_to_all(partial_out, ('ctx', 'grp'), split_axis=0, concat_axis=0,...  163 us
    all_gather x1, waiting for transfers between devices, body(): piece = lax.all_gather(local_kv, 'ctx', axis=0, tiled=True)  45.8 us
    reduce_sum x3, other arithmetic, key_block(): total = total * shrink + jnp.sum(weights, axis=-1)  29 us
    dot_general x3, matrix products, key_block(): jnp.einsum('qkgd,skd->kgqs', query_heads, keys, preferred_element_type=jn...  22.5 us
    dot_general x3, matrix products, key_block(): jnp.einsum('kgqs,skd->kgqd', weights.astype(jnp.bfloat16), values, prefer...  22.3 us
    scatter x1, local copies, waits for them, and re-layouts, body(): jnp.zeros((experts * capacity, width), jnp.bfloat16).at[dest]  16.3 us
    dot_general x1, matrix products, body(): pre = jnp.dot(flat_rows, in_weights, preferred_element_type=jnp.float32)  15.3 us
  transfers between devices with their start and end apart: 3, of which 2 were waited for; matrix products, arithmetic and copies ran while one was open for 15% of the time, Pallas kernels for 0%

commit v1 on v0

v1 whole, which is shorter than its diff:
```python
import functools
import math

import jax
import jax.numpy as jnp
from jax import lax
from jax.experimental import pallas as pl
from jax.experimental.pallas import tpu as pltpu
from jax.sharding import PartitionSpec as P

HEADS = 32
KVH = 8
HD = 64
KEY_BLOCK = 256
NEG = -1e30


def gated_act(pre, half_width):
    gate = pre[:, :half_width]
    upper = pre[:, half_width:]
    return ((upper + 1.0) * gate * jax.nn.sigmoid(1.702 * gate)).astype(jnp.bfloat16)


def attention_kernel(
    bounds, q_ref, cache_ref, stretch_ref, start_ref, sink_ref, out_ref, qs, top, total, acc
):
    tokens = q_ref.shape[0]
    pairs = KVH // 2
    per = 2 * (HEADS // KVH)
    kv_cols = KVH * HD
    cache_rows = cache_ref.shape[0]
    first_query = bounds[0]
    low = bounds[1]
    lane = lax.broadcasted_iota(jnp.int32, (tokens, 2 * HD), 1)
    lower = lane < HD
    for p in range(pairs):
        for j in range(0, per, 2):
            col = HD * (per * p + j)
            both = q_ref[:, col : col + 2 * HD].astype(jnp.float32) * (1.0 / math.sqrt(HD))
            turned = pltpu.roll(both, HD, 1)
            if j < per // 2:
                even = jnp.where(lower, both, 0.0)
                odd = jnp.where(lower, turned, 0.0)
            else:
                even = jnp.where(lower, 0.0, turned)
                odd = jnp.where(lower, 0.0, both)
            qs[p, j * tokens : (j + 1) * tokens, :] = even.astype(jnp.bfloat16)
            qs[p, (j + 1) * tokens : (j + 2) * tokens, :] = odd.astype(jnp.bfloat16)
    top[...] = sink_ref[...]
    total[...] = jnp.zeros_like(total)
    acc[...] = jnp.zeros_like(acc)
    starts = start_ref[...]
    query_pos = first_query + lax.broadcasted_iota(jnp.int32, (1, tokens), 1)

    def block(ref, row, base):
        row = pl.multiple_of(row, KEY_BLOCK)
        key_pos = base + row + lax.broadcasted_iota(jnp.int32, (KEY_BLOCK, tokens), 0)
        bias = jnp.where((key_pos >= starts) & (key_pos <= query_pos), 0.0, NEG)
        bias = jnp.concatenate([bias] * per, axis=1)
        for p in range(pairs):
            keys = ref[pl.ds(row, KEY_BLOCK), 2 * HD * p : 2 * HD * (p + 1)]
            values = ref[pl.ds(row, KEY_BLOCK), kv_cols + 2 * HD * p : kv_cols + 2 * HD * (p + 1)]
            scores = (
                lax.dot_general(
                    keys, qs[p], (((1,), (1,)), ((), ())), preferred_element_type=jnp.float32
                )
                + bias
            )
            old = top[p]
            new = jnp.maximum(old, jnp.max(scores, axis=0, keepdims=True))
            weights = jnp.exp(scores - new)
            shrink = jnp.exp(old - new)
            total[p] = total[p] * shrink + jnp.sum(weights, axis=0, keepdims=True)
            acc[p] = acc[p] * shrink + lax.dot_general(
                values,
                weights.astype(jnp.bfloat16),
                (((0,), (0,)), ((), ())),
                preferred_element_type=jnp.float32,
            )
            top[p] = new

    cache_blocks = cache_rows // KEY_BLOCK

    def cache_step(i, carry):
        block(cache_ref, i * KEY_BLOCK, 0)
        return carry

    def stretch_step(i, carry):
        block(stretch_ref, i * KEY_BLOCK, cache_rows)
        return carry

    lax.fori_loop(lax.div(low, KEY_BLOCK), cache_blocks, cache_step, 0)
    lax.fori_loop(
        lax.div(jnp.maximum(low - cache_rows, 0), KEY_BLOCK),
        lax.div(first_query + tokens - 1 - cache_rows, KEY_BLOCK) + 1,
        stretch_step,
        0,
    )
    for p in range(pairs):
        denom = total[p] + jnp.exp(sink_ref[p] - top[p])
        ready = acc[p] / denom
        for j in range(0, per, 2):
            row = 0 if j < per // 2 else HD
            upper = ready[row : row + HD, j * tokens : (j + 1) * tokens]
            under = ready[row : row + HD, (j + 1) * tokens : (j + 2) * tokens]
            col = HD * (per * p + j)
            out_ref[:, col : col + 2 * HD] = jnp.concatenate([upper, under], axis=0).T.astype(
                out_ref.dtype
            )


def attention(queries, cache_all, stretch_all, lengths, sinks, first_query):
    tokens = queries.shape[0]
    pairs = KVH // 2
    per = 2 * (HEADS // KVH)
    ends = jnp.cumsum(lengths)
    positions = first_query + jnp.arange(tokens, dtype=jnp.int32)
    starts = jnp.max(jnp.where(positions[:, None] >= ends[None, :], ends[None, :], 0), axis=1)
    bounds = jnp.stack([first_query, starts[0]]).astype(jnp.int32)
    sink_rows = jnp.repeat(sinks, tokens).reshape(pairs, 1, per * tokens)
    vmem = pl.BlockSpec(memory_space=pltpu.VMEM)
    return pl.pallas_call(
        attention_kernel,
        out_shape=jax.ShapeDtypeStruct(queries.shape, jnp.bfloat16),
        in_specs=[pl.BlockSpec(memory_space=pltpu.SMEM)] + [vmem] * 5,
        out_specs=vmem,
        scratch_shapes=[
            pltpu.VMEM((pairs, per * tokens, 2 * HD), jnp.bfloat16),
            pltpu.VMEM((pairs, 1, per * tokens), jnp.float32),
            pltpu.VMEM((pairs, 1, per * tokens), jnp.float32),
            pltpu.VMEM((pairs, 2 * HD, per * tokens), jnp.float32),
        ],
        compiler_params=pltpu.CompilerParams(vmem_limit_bytes=48 * 1024 * 1024),
        cost_estimate=pl.CostEstimate(
            flops=8_000_000_000, bytes_accessed=8_000_000, transcendentals=8_000_000
        ),
    )(bounds, queries, cache_all, stretch_all, starts[None, :].astype(jnp.int32), sink_rows)


def body(
    residual,
    queries,
    stretch_kv,
    cache_kv,
    doc_lengths,
    sinks,
    out_proj,
    norm_gain,
    router,
    expert_ids,
    expert_in,
    expert_out,
):
    tokens = residual.shape[1]
    width = residual.shape[2]
    cache_rows = cache_kv.shape[1]
    ctx_count = lax.axis_size("ctx")
    grp_count = lax.axis_size("grp")
    ctx_here = lax.axis_index("ctx")
    grp_here = lax.axis_index("grp")
    experts = router.shape[1]
    topk = expert_ids.shape[2]
    first_query = cache_rows * ctx_count + ctx_here * tokens
    cache_all = lax.all_gather(cache_kv[0], "ctx", axis=0, tiled=True)
    stretch_all = lax.all_gather(stretch_kv[0], "ctx", axis=0, tiled=True)
    proj_all = lax.all_gather(out_proj, "ctx", axis=0, tiled=True)
    ids_all = lax.all_gather(expert_ids[0], "grp", axis=0)

    plane_experts = (jnp.arange(ctx_count, dtype=jnp.int32) * grp_count + grp_here) // 2
    capacity = 2 * ((5 * tokens * topk + 8 * experts - 1) // (8 * experts))
    named = ids_all[..., None] == plane_experts
    hits = jnp.any(named, axis=2)
    before = jnp.tril(jnp.ones((tokens, tokens), jnp.bfloat16), -1)
    slots = jnp.einsum(
        "ut,gtc->guc", before, hits.astype(jnp.bfloat16), preferred_element_type=jnp.float32
    ).astype(jnp.int32)
    slots = jnp.where(hits, slots, -1)
    places = jnp.transpose(slots, (0, 2, 1))[:, :, None, :] == jnp.arange(
        capacity, dtype=jnp.int32
    )[None, None, :, None]
    places = places.reshape(grp_count, ctx_count * capacity, tokens).astype(jnp.bfloat16)

    attended = attention(
        queries[0], cache_all, stretch_all, doc_lengths[0], sinks, first_query
    )
    projected = jnp.dot(attended, proj_all, preferred_element_type=jnp.float32)
    mid = (residual[0].astype(jnp.float32) + projected).astype(jnp.bfloat16)
    mid_float = mid.astype(jnp.float32)
    normed = (
        mid_float
        * lax.rsqrt(jnp.mean(mid_float * mid_float, axis=-1, keepdims=True) + 1e-05)
        * norm_gain
    ).astype(jnp.bfloat16)
    column = lax.all_gather(normed, "grp", axis=0)
    logits = jnp.einsum("gtd,de->gte", column, router, preferred_element_type=jnp.float32)
    picks = ids_all[..., None] == jnp.arange(experts, dtype=jnp.int32)
    chosen = jnp.sum(jnp.where(picks, logits[:, :, None, :], 0.0), axis=-1)
    raised = jnp.exp(chosen)
    route_weights = raised / jnp.sum(raised, axis=-1, keepdims=True)
    by_expert = jnp.sum(jnp.where(named, route_weights[..., None], 0.0), axis=2)

    packed = jnp.einsum("gst,gtd->gsd", places, column, preferred_element_type=jnp.float32).astype(
        jnp.bfloat16
    )
    packed = jnp.transpose(packed.reshape(grp_count, ctx_count, capacity, width), (1, 0, 2, 3))
    received = lax.all_to_all(packed, "ctx", split_axis=0, concat_axis=0, tiled=True)
    in_weights = expert_in[0]
    out_weights = expert_out[0]
    pre = jnp.dot(received.reshape(-1, width), in_weights, preferred_element_type=jnp.float32)
    hidden = gated_act(pre, out_weights.shape[0])
    partial_out = jnp.dot(hidden, out_weights, preferred_element_type=jnp.float32).astype(
        jnp.bfloat16
    )
    returned = lax.all_to_all(
        partial_out.reshape(received.shape), "ctx", split_axis=0, concat_axis=0, tiled=True
    )
    places = places.reshape(grp_count, ctx_count, capacity, tokens)
    weighted = places.astype(jnp.float32) * jnp.transpose(by_expert, (0, 2, 1))[:, :, None, :]
    coarse = weighted.astype(jnp.bfloat16)
    fine = (weighted - coarse.astype(jnp.float32)).astype(jnp.bfloat16)
    mixture = jnp.einsum(
        "gcrt,cgrd->gtd", coarse, returned, preferred_element_type=jnp.float32
    ) + jnp.einsum("gcrt,cgrd->gtd", fine, returned, preferred_element_type=jnp.float32)
    sums = lax.psum_scatter(mixture.astype(jnp.bfloat16), "grp", scatter_dimension=0)
    final = (mid_float + sums.astype(jnp.float32)).astype(jnp.bfloat16)
    return (mid[None], final[None])


def solution(mesh):
    return jax.shard_map(
        body,
        mesh=mesh,
        in_specs=(
            P("grp", "ctx", None),
            P("grp", "ctx", None),
            P("grp", "ctx", None),
            P("grp", "ctx", None),
            P("grp", None),
            P(),
            P("ctx", None),
            P(),
            P(),
            P("grp", "ctx", None),
            P(("ctx", "grp"), None, None),
            P(("ctx", "grp"), None, None),
        ),
        out_specs=(P("grp", "ctx", None), P("grp", "ctx", None)),
        check_vma=False,
    )
```

time: 589 us -> 523 us (0.89); the launches traced: 579 us -> 522 us
  waiting for transfers between devices: 210 us -> 318 us
  blocking collectives: 171 us -> 101 us
  other arithmetic: 50.5 us -> 4.99 us
  local copies, waits for them, and re-layouts: 51.9 us -> 18.5 us
  matrix products: 76.5 us -> 52.6 us
  Pallas kernels: 0 us -> 7.82 us
    all_gather x2 -> x4, waiting for transfers between devices: 45.8 us -> 178 us  [the longest x1 62.4 us: body(): proj_all = lax.all_gather(out_proj, 'ctx', axis=0, tiled=True)]
    all_to_all x1, blocking collectives: 171 us -> 88.6 us  [body(): lax.all_to_all(packed, 'ctx', split_axis=0, concat_axis=0, tiled=True)]
    all_to_all x1, waiting for transfers between devices: 163 us -> 84 us  [body(): lax.all_to_all(partial_out.reshape(received.shape), 'ctx', split_axis=0,...]
    reduce_scatter x0 -> x1, waiting for transfers between devices: none -> 53.8 us  [body(): lax.psum_scatter(mixture.astype(jnp.bfloat16), 'grp', scatter_dimension=0)]
    reduce_sum x11 -> x2, other arithmetic: 43.9 us -> 0.13 us  [the longest x1 0.08 us: body(): by_expert = jnp.sum(jnp.where(named, route_weights[..., None], 0.0), axis=2)]
    dot_general x9 -> x7, matrix products: 68.1 us -> 44.3 us  [the longest x1 15.3 us: body(): jnp.dot(received.reshape(-1, width), in_weights, preferred_element_type=j...]
    scatter x1 -> x0, local copies, waits for them, and re-layouts: 16.3 us -> none  [body(): jnp.zeros((experts * capacity, width), jnp.bfloat16).at[dest]]
    all_gather x0 -> x1, blocking collectives: none -> 12.1 us  [body(): ids_all = lax.all_gather(expert_ids[0], 'grp', axis=0)]
  transfers between devices with their start and end apart: 3 -> 6, of which waited for: 2 -> 6; matrix products, arithmetic and copies ran while one was open for 15% -> 1% of each run, Pallas kernels for 0% -> 1%
where the time goes in v1:
time: 523 us; the launch traced here: 522 us
  waiting for transfers between devices  318 us (61%)
  blocking collectives  101 us (19%)
  matrix products  52.6 us (10%)
  local copies, waits for them, and re-layouts  18.5 us (4%)
  between operations  14 us (3%)
  Pallas kernels  7.82 us (1%)
  starting transfers between devices  5.55 us (1%)
    all_to_all x1, blocking collectives, body(): lax.all_to_all(packed, 'ctx', split_axis=0, concat_axis=0, tiled=True)  88.6 us
    all_to_all x1, waiting for transfers between devices, body(): lax.all_to_all(partial_out.reshape(received.shape), 'ctx', split_axis=0,...  84 us
    all_gather x1, waiting for transfers between devices, body(): proj_all = lax.all_gather(out_proj, 'ctx', axis=0, tiled=True)  62.4 us
    reduce_scatter x1, waiting for transfers between devices, body(): lax.psum_scatter(mixture.astype(jnp.bfloat16), 'grp', scatter_dimension=0)  53.8 us
    all_gather x1, waiting for transfers between devices, body(): column = lax.all_gather(normed, 'grp', axis=0)  47.7 us
    all_gather x1, waiting for transfers between devices, body(): cache_all = lax.all_gather(cache_kv[0], 'ctx', axis=0, tiled=True)  38.6 us
    all_gather x1, waiting for transfers between devices, body(): stretch_all = lax.all_gather(stretch_kv[0], 'ctx', axis=0, tiled=True)  29.3 us
    dot_general x1, matrix products, body(): jnp.dot(received.reshape(-1, width), in_weights, preferred_element_type=j...  15.3 us
  transfers between devices with their start and end apart: 6, of which 6 were waited for; matrix products, arithmetic and copies ran while one was open for 1% of the time, Pallas kernels for 1%

profile of v1, /device:TPU:0, one launch (start us, length us, event | category | flops | bytes accessed | tf_op | source)
XLA Modules:
  0.0 522.0 jit_solution(1078680778062522977)
XLA Ops:
  7.2 0.0 copy-start
  7.2 0.0 all-gather.12.cloned.1.call-start
  7.2 0.7 all-gather.12.cloned.1.call-update
  7.9 0.0 all-gather.10.cloned.1.call-start
  8.0 0.7 all-gather.10.cloned.1.call-update
  8.7 0.0 all-gather.8.cloned.1.call-start
  8.7 0.7 all-gather.8.cloned.1.call-update
  9.4 0.0 all-gather.14.cloned.1.call-start
  9.4 0.7 broadcast_in_dim.78
  10.2 0.8 reduce-window.8
  11.0 0.1 select_reduce_fusion.1
  11.1 0.1 pad_add_fusion.bounds
  11.2 29.3 %all-gather.12.cloned.1.call-done = bf16[1,1024,1024]{2,1,0:T(8,128)(2,1)} async-done(((bf16[1,128,1024]{2,1,0:T(8,128)(2,1)}), bf16[1,1024,1024]{2,1,0:T(8,128)(2,1)}) %all-gather.12.cloned.1.call-update) | async-done | bytes 2097168 | tf_op jit(solution)/shard_map/all_gather | solution.py:165
  40.6 38.6 %all-gather.10.cloned.1.call-done = bf16[1,2048,1024]{2,1,0:T(8,128)(2,1)} async-done(((bf16[1,256,1024]{2,1,0:T(8,128)(2,1)}), bf16[1,2048,1024]{2,1,0:T(8,128)(2,1)}) %all-gather.10.cloned.1.call-update) | async-done | bytes 4194320 | tf_op jit(solution)/shard_map/all_gather | solution.py:164
  79.2 0.1 broadcast_in_dim.79
  79.3 1.6 copy-done.1
  80.9 1.0 copy-done.2
  81.9 7.8 %shard_map.131 = bf16[128,2048]{1,0:T(8,128)(2,1)S(1)} custom-call(s32[2]{0:T(128)S(1)} %pad_add_fusion.bounds, bf16[128,2048]{1,0:T(8,128)(2,1)S(1)} %bitcast.68, bf16[2048,1024]{1,0:T(8,128)(2,1)} %bitcast.80, bf16[1024,1024]{1,0:T(8,128)(2,1)S(1)} %bitcast.67, s32[1,128]{1,0:T(1,128)S(1)} %bitcast.70, f32[4,1,1024]{2,1,0:T(1,128)S(1)} %bitcast.66), custom_call_target="tpu_custom_call" | custom-call | flops 8000000000 | bytes 8000000 | tf_op jit(solution)/shard_map/pallas_call | solution.py:122
  89.7 0.0 copy-start.7
  89.7 62.4 %all-gather.8.cloned.1.call-done = bf16[2048,2880]{0,1:T(8,128)(2,1)} async-done(((bf16[256,2880]{0,1:T(8,128)(2,1)}), bf16[2048,2880]{0,1:T(8,128)(2,1)}) %all-gather.8.cloned.1.call-update) | async-done | bytes 11796496 | tf_op jit(solution)/shard_map/all_gather | solution.py:166
  152.2 7.6 %fusion.22 = (f32[128]{0:T(128)S(1)}, bf16[128,2880]{0,1:T(8,128)(2,1)S(1)}) fusion(bf16[128,2048]{1,0:T(8,128)(2,1)S(1)} %shard_map.131, bf16[2048,2880]{0,1:T(8,128)(2,1)} %all-gather.8.cloned.1.call-done, bf16[1,128,2880]{1,2,0:T(8,128)(2,1)S(1)} %copy-done.6), kind=kOutput, calls=%fused_computation.28 | convolution fusion | flops 1512161152 | bytes 13795840 | tf_op jit(solution)/shard_map/dot_general | solution.py:186
  159.8 0.8 copy-done.4
  160.7 1.3 fusion.24
  162.0 0.0 all-gather.14.cloned.1.call-update
  162.0 0.1 eq.62
  162.1 12.1 %all_gather.21 = s32[4,128,4]{1,2,0:T(4,128)S(1)} all-gather(s32[1,128,4]{1,2,0:T(4,128)S(1)} %copy-done.8), channel_id=1, replica_groups=mesh['ctx'=8,'grp'=4] {'grp'}, dimensions={0}, use_global_device_ids=true | all-gather | bytes 10240 | tf_op jit(solution)/shard_map/all_gather | solution.py:167
  174.2 0.1 compare_reduce_fusion
  174.3 0.2 fusion.26
  174.5 0.2 bitcast_compare_fusion
  174.7 47.7 %all-gather.14.cloned.1.call-done = bf16[512,2880]{0,1:T(8,128)(2,1)} async-done(((bf16[128,2880]{0,1:T(8,128)(2,1)}), bf16[512,2880]{0,1:T(8,128)(2,1)}) %all-gather.14.cloned.1.call-update) | async-done | bytes 2949136 | tf_op jit(solution)/shard_map/all_gather | solution.py:194
  222.4 6.9 %convolution_convert_fusion.1 = bf16[4,320,2880]{2,1,0:T(8,128)(2,1)} fusion(pred[4,320,128]{2,1,0:T(32,128)(4,1)S(1)} %bitcast_compare_fusion, bf16[512,2880]{0,1:T(8,128)(2,1)} %all-gather.14.cloned.1.call-done), kind=kOutput, calls=%fused_computation.8 | convolution fusion | flops 947404800 | bytes 10485760 | tf_op jit(solution)/shard_map/gst,gtd->gsd/dot_general | solution.py:202
  229.3 3.7 copy.61
  233.0 0.0 slice-start
  233.0 88.6 %all_to_all.10 = bf16[8,4,40,2880]{3,2,1,0:T(8,128)(2,1)S(1)} all-to-all(bf16[8,4,40,2880]{3,2,1,0:T(8,128)(2,1)S(1)} %bitcast.72), channel_id=1, replica_groups=mesh['ctx'=8,'grp'=4] {'ctx'}, dimensions={0} | all-to-all | bytes 14745600 | tf_op jit(solution)/shard_map/all_to_all | solution.py:206
  321.6 15.3 %fusion = f32[1280,1536]{1,0:T(8,128)S(1)} fusion(bf16[1280,2880]{1,0:T(8,128)(2,1)S(1)} %bitcast.74, bf16[1,2880,1536]{2,1,0:T(8,128)(2,1)} %param.22), kind=kOutput, calls=%fused_computation.1 | convolution fusion | flops 11324620800 | bytes 24084480 | tf_op jit(solution)/shard_map/dot_general | solution.py:209
  336.9 8.3 %convolution_convert_fusion = bf16[1280,2880]{0,1:T(8,128)(2,1)} fusion(bf16[1,768,2880]{1,2,0:T(8,128)(2,1)S(1)} %bitcast.79, f32[1280,1536]{1,0:T(8,128)S(1)} %fusion), kind=kOutput, calls=%fused_computation | convolution fusion | flops 5673861120 | bytes 19660800 | tf_op jit(solution)/shard_map/dot_general | solution.py:211
  345.2 10.5 %copy.40 = bf16[1280,2880]{1,0:T(8,128)(2,1)} copy(bf16[1280,2880]{0,1:T(8,128)(2,1)} %convolution_convert_fusion) | data formatting | bytes 14745600 | tf_op jit(solution)/shard_map/convert_element_type | solution.py:211
  355.7 5.1 all-to-all-start.1
  360.9 0.3 reduce-scatter.2.cloned.1.call-start
  361.1 0.5 fusion.15
  361.7 0.1 fusion.36
  361.8 84.0 %all-to-all-done.1 = bf16[8,4,40,2880]{3,2,1,0:T(8,128)(2,1)} async-done(((bf16[8,4,40,2880]{3,2,1,0:T(8,128)(2,1)}), bf16[8,4,40,2880]{3,2,1,0:T(8,128)(2,1)}, u32[]{:S(2)}, u32[]{:S(2)}) %all-to-all-start.1) | async-done | bytes 7372832 | tf_op jit(solution)/shard_map/all_to_all | solution.py:214
  445.8 5.8 %fusion.2 = f32[4,128,2880,1]{1,2,3,0:T(8,128)S(1)} fusion(bf16[8,4,40,2880]{3,2,1,0:T(8,128)(2,1)} %all-to-all-done.1, f32[4,8,128]{2,1,0:T(8,128)S(1)} %bitcast.76, s32[4,8,128]{2,1,0:T(8,128)S(1)} %fusion.26), kind=kOutput, calls=%fused_computation.4 | convolution fusion | flops 945029120 | bytes 13303808 | tf_op jit(solution)/shard_map/gcrt,cgrd->gtd/dot_general | solution.py:223
  451.6 0.0 copy-start.5
  451.6 7.9 %fusion.6 = bf16[4,128,2880]{1,2,0:T(8,128)(2,1)} fusion(f32[4,128,2880,1]{1,2,3,0:T(8,128)S(1)} %fusion.2, bf16[8,4,40,2880]{3,2,1,0:T(8,128)(2,1)} %all-to-all-done.1, f32[4,8,128]{2,1,0:T(8,128)S(1)} %bitcast.77, s32[4,8,128]{2,1,0:T(8,128)S(1)} %fusion.26), kind=kOutput, calls=%fused_computation.10 | convolution fusion | flops 947486720 | bytes 16252928 | tf_op jit(solution)/shard_map/gcrt,cgrd->gtd/dot_general | solution.py:221
  459.5 0.0 reduce-scatter.2.cloned.1.call-update
  459.5 53.8 %reduce-scatter.2.cloned.1.call-done = bf16[1,128,2880]{1,2,0:T(8,128)(2,1)} async-done(((bf16[4,128,2880]{1,2,0:T(8,128)(2,1)}), bf16[1,128,2880]{1,2,0:T(8,128)(2,1)}) %reduce-scatter.2.cloned.1.call-update) | async-done | bytes 737296 | tf_op jit(solution)/shard_map/reduce_scatter | solution.py:224
  513.3 2.2 fusion.27
  (24 shorter events, 0.1 us)
Async XLA Ops:
  7.2 354.0 %copy-start = (bf16[2880,16]{0,1:T(8,128)(2,1)S(1)}, bf16[2880,16]{0,1:T(8,128)(2,1)}, u32[]{:S(2)}) copy-start(bf16[2880,16]{0,1:T(8,128)(2,1)} %param.20) | copy-start | bytes 276484
  7.2 33.4 %all-gather.12.cloned.1.call-start = ((), (), s32[]{:S(2)}) async-start(), calls=%async_computation.6 | async-start | bytes 2359296 | tf_op jit(solution)/shard_map/all_gather | solution.py:165
  7.9 71.3 %all-gather.10.cloned.1.call-start = ((), (), s32[]{:S(2)}) async-start(), calls=%async_computation.5 | async-start | bytes 4718592 | tf_op jit(solution)/shard_map/all_gather | solution.py:164
  8.7 143.5 %all-gather.8.cloned.1.call-start = ((), (), s32[]{:S(2)}) async-start(), calls=%async_computation.3 | async-start | bytes 13271040 | tf_op jit(solution)/shard_map/all_gather | solution.py:166
  9.4 213.0 %all-gather.14.cloned.1.call-start = ((), (), s32[]{:S(2)}) async-start(), calls=%async_computation.7 | async-start | bytes 3686400 | tf_op jit(solution)/shard_map/all_gather | solution.py:194
  79.3 1.6 copy-start.1
  80.9 1.0 copy-start.2
  81.9 70.3 %copy-start.6 = (bf16[1,128,2880]{1,2,0:T(8,128)(2,1)S(1)}, bf16[1,128,2880]{1,2,0:T(8,128)(2,1)}, u32[]{:S(2)}) copy-start(bf16[1,128,2880]{1,2,0:T(8,128)(2,1)} %param.12) | copy-start | bytes 2211844
  89.7 70.9 %copy-start.7 = (f32[2880]{0:T(1024)S(1)}, f32[2880]{0:T(1024)}, u32[]{:S(2)}) copy-start(f32[2880]{0:T(1024)} %param.19) | copy-start | bytes 34564
  89.7 72.3 %copy-start.8 = (s32[1,128,4]{1,2,0:T(4,128)S(1)}, s32[1,128,4]{1,2,0:T(4,128)}, u32[]{:S(2)}) copy-start(s32[1,128,4]{1,2,0:T(4,128)} %param.21) | copy-start | bytes 6148
  159.8 0.9 copy-start.4
  233.0 103.9 %slice-start = ((s8[4423680]{0:T(1024)(128)(4,1)}), s8[4194304]{0:T(1024)(128)(4,1)S(1)}, s32[]{:S(2)}) async-start(s8[4423680]{0:T(1024)(128)(4,1)} %bitcast.78), calls=%async_computation.8 | async-start | bytes 8388608
  321.6 15.3 %slice-start.1 = ((s8[4423680]{0:T(1024)(128)(4,1)}), s8[229376]{0:T(1024)(128)(4,1)S(1)}, s32[]{:S(2)}) async-start(s8[4423680]{0:T(1024)(128)(4,1)} %bitcast.78), calls=%async_computation.9 | async-start | bytes 458752
  355.7 5.4 %copy-start.3 = (bf16[512,2880]{0,1:T(8,128)(2,1)S(1)}, bf16[512,2880]{0,1:T(8,128)(2,1)}, u32[]{:S(2)}) copy-start(bf16[512,2880]{0,1:T(8,128)(2,1)} %all-gather.14.cloned.1.call-done) | copy-start | bytes 8847364
  355.7 90.1 %all-to-all-start.1 = ((bf16[8,4,40,2880]{3,2,1,0:T(8,128)(2,1)}), bf16[8,4,40,2880]{3,2,1,0:T(8,128)(2,1)}, u32[]{:S(2)}, u32[]{:S(2)}) async-start(bf16[8,4,40,2880]{3,2,1,0:T(8,128)(2,1)} %bitcast.71), calls=%async_computation.1 | async-start | bytes 15073280 | tf_op jit(solution)/shard_map/all_to_all | solution.py:214
  360.9 152.4 %reduce-scatter.2.cloned.1.call-start = ((), (), s32[]{:S(2)}) async-start(), calls=%async_computation.4 | async-start | bytes 3686400 | tf_op jit(solution)/shard_map/reduce_scatter | solution.py:224
  451.6 61.7 %copy-start.5 = (bf16[128,2880]{0,1:T(8,128)(2,1)S(1)}, bf16[128,2880]{0,1:T(8,128)(2,1)}, u32[]{:S(2)}) copy-start(bf16[128,2880]{0,1:T(8,128)(2,1)} %copy-done.4) | copy-start | bytes 2211844
Sparse Core Ops, SparseCore 0:
  9.9 30.6 all-gather.11
  42.4 36.7 all-gather.9
  81.1 71.0 all-gather.7
  162.1 60.1 all-gather.13
  459.6 53.6 reduce-scatter.1

commit v2 on v1

v2 whole, which is shorter than its diff:
```python
import functools
import math

import jax
import jax.numpy as jnp
from jax import lax
from jax.experimental import pallas as pl
from jax.experimental.pallas import tpu as pltpu
from jax.sharding import PartitionSpec as P

HEADS = 32
KVH = 8
HD = 64
KEY_BLOCK = 256
NEG = -1e30


def gated_act(pre, half_width):
    gate = pre[:, :half_width]
    upper = pre[:, half_width:]
    return ((upper + 1.0) * gate * jax.nn.sigmoid(1.702 * gate)).astype(jnp.bfloat16)


def attention_kernel(
    cache_rows, stretch_rows, lows, recv_ref, start_ref, sink_ref, out_ref, qs, top, total, acc
):
    sources = recv_ref.shape[0]
    span = cache_rows + stretch_rows
    tokens = stretch_rows
    heads = sink_ref.shape[1] // tokens
    cache_total = sources * cache_rows
    lower = lax.broadcasted_iota(jnp.int32, (tokens, 2 * HD), 1) < HD
    cache_per = KEY_BLOCK // cache_rows
    stretch_per = KEY_BLOCK // stretch_rows

    def query_block(b, carry):
        for j in range(0, heads, 2):
            first = span + j // 2 * tokens
            both = recv_ref[b, first : first + tokens, :].astype(jnp.float32)
            both = both * (1.0 / math.sqrt(HD))
            even = jnp.where(lower, both, 0.0)
            odd = jnp.where(lower, pltpu.roll(both, HD, 1), 0.0)
            qs[j * tokens : (j + 1) * tokens, :] = even.astype(jnp.bfloat16)
            qs[(j + 1) * tokens : (j + 2) * tokens, :] = odd.astype(jnp.bfloat16)
        top[...] = sink_ref[...]
        total[...] = jnp.zeros_like(total)
        acc[...] = jnp.zeros_like(acc)
        starts = start_ref[b]
        query_pos = cache_total + b * tokens + lax.broadcasted_iota(jnp.int32, (1, tokens), 1)
        low = lows[b]

        def block(keys_values, base):
            key_pos = base + lax.broadcasted_iota(jnp.int32, (KEY_BLOCK, tokens), 0)
            bias = jnp.where((key_pos >= starts) & (key_pos <= query_pos), 0.0, NEG)
            bias = jnp.concatenate([bias, bias], axis=1)
            for j in range(0, heads, 2):
                cols = slice(j * tokens, (j + 2) * tokens)
                scores = (
                    lax.dot_general(
                        keys_values,
                        qs[cols, :],
                        (((1,), (1,)), ((), ())),
                        preferred_element_type=jnp.float32,
                    )
                    + bias
                )
                old = top[:, cols]
                new = jnp.maximum(old, jnp.max(scores, axis=0, keepdims=True))
                weights = jnp.exp(scores - new)
                shrink = jnp.exp(old - new)
                total[:, cols] = total[:, cols] * shrink + jnp.sum(weights, axis=0, keepdims=True)
                acc[:, cols] = acc[:, cols] * shrink + lax.dot_general(
                    keys_values,
                    weights.astype(jnp.bfloat16),
                    (((0,), (0,)), ((), ())),
                    preferred_element_type=jnp.float32,
                )
                top[:, cols] = new

        def cache_step(i, inner):
            parts = [recv_ref[i * cache_per + k, :cache_rows, :] for k in range(cache_per)]
            block(jnp.concatenate(parts, axis=0), i * KEY_BLOCK)
            return inner

        def stretch_step(i, inner):
            parts = [
                recv_ref[i * stretch_per + k, cache_rows:span, :] for k in range(stretch_per)
            ]
            block(jnp.concatenate(parts, axis=0), cache_total + i * KEY_BLOCK)
            return inner

        lax.fori_loop(lax.div(low, KEY_BLOCK), cache_total // KEY_BLOCK, cache_step, 0)
        lax.fori_loop(
            lax.div(jnp.maximum(low - cache_total, 0), KEY_BLOCK),
            lax.div(b * tokens + tokens - 1, KEY_BLOCK) + 1,
            stretch_step,
            0,
        )
        denom = total[...] + jnp.exp(sink_ref[...] - top[...])
        ready = acc[HD:, :] / denom
        for j in range(0, heads, 2):
            pair = jnp.concatenate(
                [ready[:, j * tokens : (j + 1) * tokens], ready[:, (j + 1) * tokens : (j + 2) * tokens]],
                axis=0,
            )
            out_ref[b, :, j * HD : (j + 2) * HD] = pair.T.astype(out_ref.dtype)
        return carry

    lax.fori_loop(0, sources, query_block, 0)


def attention(queries, stretch_kv, cache_kv, lengths, sinks, ctx_here, ctx_count):
    tokens = queries.shape[0]
    cache_rows = cache_kv.shape[0]
    heads = HEADS // ctx_count
    local = jnp.concatenate([cache_kv, stretch_kv], axis=0)
    span = local.shape[0]
    local = local.reshape(span, 2, KVH, HD).transpose(2, 0, 1, 3).reshape(KVH, span, 2 * HD)
    local = jnp.repeat(local, ctx_count // KVH, axis=0)
    asked = queries.reshape(tokens, ctx_count, heads // 2, 2 * HD).transpose(1, 2, 0, 3)
    asked = asked.reshape(ctx_count, heads // 2 * tokens, 2 * HD)
    sent = jnp.concatenate([local, asked], axis=1)
    recv = lax.all_to_all(sent, "ctx", split_axis=0, concat_axis=0, tiled=True)
    ends = jnp.cumsum(lengths)
    positions = cache_rows * ctx_count + jnp.arange(ctx_count * tokens, dtype=jnp.int32)
    starts = jnp.max(jnp.where(positions[:, None] >= ends[None, :], ends[None, :], 0), axis=1)
    starts = starts.astype(jnp.int32).reshape(ctx_count, 1, tokens)
    own_sinks = lax.dynamic_slice_in_dim(sinks, ctx_here * heads, heads, 0)
    sink_row = jnp.repeat(own_sinks, tokens)[None, :]
    vmem = pl.BlockSpec(memory_space=pltpu.VMEM)
    attended = pl.pallas_call(
        functools.partial(attention_kernel, cache_rows, tokens),
        out_shape=jax.ShapeDtypeStruct((ctx_count, tokens, heads * HD), jnp.bfloat16),
        in_specs=[pl.BlockSpec(memory_space=pltpu.SMEM)] + [vmem] * 3,
        out_specs=vmem,
        scratch_shapes=[
            pltpu.VMEM((heads * tokens, 2 * HD), jnp.bfloat16),
            pltpu.VMEM((1, heads * tokens), jnp.float32),
            pltpu.VMEM((1, heads * tokens), jnp.float32),
            pltpu.VMEM((2 * HD, heads * tokens), jnp.float32),
        ],
        compiler_params=pltpu.CompilerParams(vmem_limit_bytes=32 * 1024 * 1024),
        cost_estimate=pl.CostEstimate(
            flops=8_000_000_000, bytes_accessed=2_000_000, transcendentals=8_000_000
        ),
    )(starts[:, 0, 0], recv, starts, sink_row)
    back = lax.all_to_all(attended, "ctx", split_axis=0, concat_axis=0, tiled=True)
    return back.transpose(1, 0, 2).reshape(tokens, HEADS * HD)


def body(
    residual,
    queries,
    stretch_kv,
    cache_kv,
    doc_lengths,
    sinks,
    out_proj,
    norm_gain,
    router,
    expert_ids,
    expert_in,
    expert_out,
):
    tokens = residual.shape[1]
    width = residual.shape[2]
    ctx_count = lax.axis_size("ctx")
    grp_count = lax.axis_size("grp")
    ctx_here = lax.axis_index("ctx")
    grp_here = lax.axis_index("grp")
    experts = router.shape[1]
    topk = expert_ids.shape[2]
    proj_all = lax.all_gather(out_proj, "ctx", axis=0, tiled=True)
    ids_all = lax.all_gather(expert_ids[0], "grp", axis=0)

    plane_experts = (jnp.arange(ctx_count, dtype=jnp.int32) * grp_count + grp_here) // 2
    capacity = 2 * ((5 * tokens * topk + 8 * experts - 1) // (8 * experts))
    named = ids_all[..., None] == plane_experts
    hits = jnp.any(named, axis=2)
    before = jnp.tril(jnp.ones((tokens, tokens), jnp.bfloat16), -1)
    slots = jnp.einsum(
        "ut,gtc->guc", before, hits.astype(jnp.bfloat16), preferred_element_type=jnp.float32
    ).astype(jnp.int32)
    slots = jnp.where(hits, slots, -1)
    places = jnp.transpose(slots, (0, 2, 1))[:, :, None, :] == jnp.arange(
        capacity, dtype=jnp.int32
    )[None, None, :, None]
    places = jnp.transpose(
        places.reshape(grp_count, ctx_count, capacity, tokens), (1, 0, 2, 3)
    )
    same = jnp.eye(grp_count, dtype=jnp.bool_)[None, :, None, :, None]
    spread = (places[:, :, :, None, :] & same).reshape(-1, grp_count * tokens)

    attended = attention(
        queries[0], stretch_kv[0], cache_kv[0], doc_lengths[0], sinks, ctx_here, ctx_count
    )
    projected = jnp.dot(attended, proj_all, preferred_element_type=jnp.float32)
    mid = (residual[0].astype(jnp.float32) + projected).astype(jnp.bfloat16)
    mid_float = mid.astype(jnp.float32)
    normed = (
        mid_float
        * lax.rsqrt(jnp.mean(mid_float * mid_float, axis=-1, keepdims=True) + 1e-05)
        * norm_gain
    ).astype(jnp.bfloat16)
    column = lax.all_gather(normed, "grp", axis=0)
    logits = jnp.einsum("gtd,de->gte", column, router, preferred_element_type=jnp.float32)
    picks = ids_all[..., None] == jnp.arange(experts, dtype=jnp.int32)
    chosen = jnp.sum(jnp.where(picks, logits[:, :, None, :], 0.0), axis=-1)
    raised = jnp.exp(chosen)
    route_weights = raised / jnp.sum(raised, axis=-1, keepdims=True)
    by_expert = jnp.sum(jnp.where(named, route_weights[..., None], 0.0), axis=2)

    packed = jnp.dot(
        spread.astype(jnp.bfloat16),
        column.reshape(-1, width),
        preferred_element_type=jnp.float32,
    ).astype(jnp.bfloat16)
    packed = packed.reshape(ctx_count, grp_count * capacity, width)
    received = lax.all_to_all(packed, "ctx", split_axis=0, concat_axis=0, tiled=True)
    in_weights = expert_in[0]
    out_weights = expert_out[0]
    pre = jnp.dot(received.reshape(-1, width), in_weights, preferred_element_type=jnp.float32)
    hidden = gated_act(pre, out_weights.shape[0])
    partial_out = jnp.dot(hidden, out_weights, preferred_element_type=jnp.float32).astype(
        jnp.bfloat16
    )
    returned = lax.all_to_all(
        partial_out.reshape(received.shape), "ctx", split_axis=0, concat_axis=0, tiled=True
    )
    scale = jnp.transpose(by_expert, (2, 0, 1))[:, :, None, :]
    weighted = jnp.where(places, scale, 0.0).astype(jnp.bfloat16)[:, :, :, None, :]
    weighted = jnp.where(same, weighted, jnp.zeros_like(weighted)).reshape(spread.shape)
    mixture = lax.dot_general(
        weighted,
        returned.reshape(-1, width),
        (((0,), (0,)), ((), ())),
        preferred_element_type=jnp.float32,
    ).reshape(grp_count, tokens, width)
    sums = lax.psum_scatter(mixture.astype(jnp.bfloat16), "grp", scatter_dimension=0)
    final = (mid_float + sums.astype(jnp.float32)).astype(jnp.bfloat16)
    return (mid[None], final[None])


def solution(mesh):
    return jax.shard_map(
        body,
        mesh=mesh,
        in_specs=(
            P("grp", "ctx", None),
            P("grp", "ctx", None),
            P("grp", "ctx", None),
            P("grp", "ctx", None),
            P("grp", None),
            P(),
            P("ctx", None),
            P(),
            P(),
            P("grp", "ctx", None),
            P(("ctx", "grp"), None, None),
            P(("ctx", "grp"), None, None),
        ),
        out_specs=(P("grp", "ctx", None), P("grp", "ctx", None)),
        check_vma=False,
    )
```

time: 523 us -> 474 us (0.906)
  waiting for transfers between devices: 318 us -> 217 us
  Pallas kernels: 7.82 us -> 30.5 us
  blocking collectives: 101 us -> 119 us
  local copies, waits for them, and re-layouts: 18.5 us -> 26.6 us
    all_gather x2 -> x0, waiting for transfers between devices: 68 us -> none  [the longest x1 38.6 us: body(): cache_all = lax.all_gather(cache_kv[0], 'ctx', axis=0, tiled=True)]
    all_gather x1, waiting for transfers between devices: 62.4 us -> 3.85 us  [body(): proj_all = lax.all_gather(out_proj, 'ctx', axis=0, tiled=True)]
    all_to_all x0 -> x1, waiting for transfers between devices: none -> 29.2 us  [attention(): recv = lax.all_to_all(sent, 'ctx', split_axis=0, concat_axis=0, tiled=True)]
    pallas_call x1, Pallas kernels: 7.82 us -> 30.5 us  [attention(): pl.pallas_call(functools.partial(attention_kernel, cache_rows, tokens), o...]
    all_to_all x0 -> x1, blocking collectives: none -> 18.1 us  [attention(): lax.all_to_all(attended, 'ctx', split_axis=0, concat_axis=0, tiled=True)]
    convert_element_type x0 -> x1, local copies, waits for them, and re-layouts: none -> 10.4 us  [body(): packed = jnp.dot(spread.astype(jnp.bfloat16), column.reshape(-1, width),...]
    dot_general x3 -> x2, matrix products: 20.6 us -> 16.5 us  [the longest x1 8.74 us: body(): jnp.dot(spread.astype(jnp.bfloat16), column.reshape(-1, width), preferred...]
  transfers between devices with their start and end apart: 6 -> 5, of which waited for: 6 -> 5; matrix products, arithmetic and copies ran while one was open for 1% -> 2% of each run, Pallas kernels for 1% -> 6%
where the time goes in v2:
time: 474 us; the launch traced here: 473 us
  waiting for transfers between devices  217 us (46%)
  blocking collectives  119 us (25%)
  matrix products  48.5 us (10%)
  Pallas kernels  30.5 us (6%)
  local copies, waits for them, and re-layouts  26.6 us (6%)
  between operations  14 us (3%)
  starting transfers between devices  10.6 us (2%)
  other arithmetic  7.1 us (1%)
    all_to_all x1, blocking collectives, body(): lax.all_to_all(packed, 'ctx', split_axis=0, concat_axis=0, tiled=True)  88.9 us
    all_to_all x1, waiting for transfers between devices, body(): lax.all_to_all(partial_out.reshape(received.shape), 'ctx', split_axis=0,...  82.3 us
    reduce_scatter x1, waiting for transfers between devices, body(): lax.psum_scatter(mixture.astype(jnp.bfloat16), 'grp', scatter_dimension=0)  53.8 us
    all_gather x1, waiting for transfers between devices, body(): column = lax.all_gather(normed, 'grp', axis=0)  47.1 us
    pallas_call x1, Pallas kernels, attention(): pl.pallas_call(functools.partial(attention_kernel, cache_rows, tokens), o...  30.5 us
    all_to_all x1, waiting for transfers between devices, attention(): recv = lax.all_to_all(sent, 'ctx', split_axis=0, concat_axis=0, tiled=True)  29.2 us
    all_to_all x1, blocking collectives, attention(): lax.all_to_all(attended, 'ctx', split_axis=0, concat_axis=0, tiled=True)  18.1 us
    dot_general x1, matrix products, body(): jnp.dot(received.reshape(-1, width), in_weights, preferred_element_type=j...  15.3 us
  transfers between devices with their start and end apart: 5, of which 5 were waited for; matrix products, arithmetic and copies ran while one was open for 2% of the time, Pallas kernels for 6%

profile of v2, /device:TPU:0, one launch (start us, length us, event | category | flops | bytes accessed | tf_op | source)
XLA Modules:
  0.0 473.4 jit_solution(16165646847920614174)
XLA Ops:
  7.2 0.0 all-gather.4.cloned.1.call-start
  7.2 0.7 all-gather.4.cloned.1.call-update
  7.9 1.1 copy.53
  9.0 1.4 reshape_squeeze.3
  10.5 0.1 copy.55
  10.6 0.2 copy.52
  10.8 0.1 maximum_bitcast_fusion
  10.9 0.1 copy.54
  11.0 0.4 copy.56
  11.4 1.2 pad_maximum_fusion
  12.6 5.2 %all-to-all-start = ((bf16[8,640,128]{2,1,0:T(8,128)(2,1)}), bf16[8,640,128]{2,1,0:T(8,128)(2,1)S(1)}, u32[]{:S(2)}, u32[]{:S(2)}) async-start(bf16[8,640,128]{2,1,0:T(8,128)(2,1)} %pad_maximum_fusion), calls=%async_computation | async-start | bytes 2621440 | tf_op jit(solution)/shard_map/all_to_all | solution.py:123
  17.9 0.2 reduce-window.8
  18.1 0.1 dynamic_slice.3
  18.1 0.1 select_reduce_fusion.1
  18.2 0.2 slice_reduce_fusion.lows
  18.5 29.2 %all-to-all-done.recv_ref = bf16[8,640,128]{2,1,0:T(8,128)(2,1)S(1)} async-done(((bf16[8,640,128]{2,1,0:T(8,128)(2,1)}), bf16[8,640,128]{2,1,0:T(8,128)(2,1)S(1)}, u32[]{:S(2)}, u32[]{:S(2)}) %all-to-all-start) | async-done | bytes 1310752 | tf_op jit(solution)/shard_map/all_to_all | solution.py:123
  47.7 0.1 broadcast_in_dim.112
  47.7 30.5 %shard_map.131 = bf16[8,128,256]{2,1,0:T(8,128)(2,1)S(1)} custom-call(s32[8]{0:T(128)S(1)} %slice_reduce_fusion.lows, bf16[8,640,128]{2,1,0:T(8,128)(2,1)S(1)} %all-to-all-done.recv_ref, s32[8,1,128]{2,1,0:T(1,128)S(1)} %bitcast.77, f32[1,512]{1,0:T(1,128)S(1)} %bitcast.78), custom_call_target="tpu_custom_call" | custom-call | flops 8000000000 | bytes 2000000 | tf_op jit(solution)/shard_map/pallas_call | solution.py:131
  78.3 18.1 %all_to_all.20 = bf16[8,128,256]{2,1,0:T(8,128)(2,1)S(1)} all-to-all(bf16[8,128,256]{2,1,0:T(8,128)(2,1)S(1)} %shard_map.131), channel_id=1, replica_groups=mesh['ctx'=8,'grp'=4] {'ctx'}, dimensions={0} | all-to-all | bytes 1048576 | tf_op jit(solution)/shard_map/all_to_all | solution.py:147
  96.4 0.3 copy.57
  96.6 3.9 all-gather.4.cloned.1.call-done
  100.5 7.7 %fusion.15 = (f32[128]{0:T(128)S(1)}, bf16[128,2880]{0,1:T(8,128)(2,1)S(1)}) fusion(bf16[2048,2880]{0,1:T(8,128)(2,1)} %all-gather.4.cloned.1.call-done, bf16[128,2048]{0,1:T(8,128)(2,1)S(1)} %bitcast.92, bf16[1,128,2880]{1,2,0:T(8,128)(2,1)S(1)} %copy-done.7), kind=kOutput, calls=%fused_computation.22 | convolution fusion | flops 1512161152 | bytes 13795840 | tf_op jit(solution)/shard_map/dot_general | solution.py:197
  108.2 0.8 copy-done.2
  109.0 1.3 fusion.17
  110.4 12.0 %all_gather.13 = s32[4,128,4]{1,2,0:T(4,128)S(1)} all-gather(s32[1,128,4]{1,2,0:T(4,128)S(1)} %copy-done.6), channel_id=1, replica_groups=mesh['ctx'=8,'grp'=4] {'grp'}, dimensions={0}, use_global_device_ids=true | all-gather | bytes 10240 | tf_op jit(solution)/shard_map/all_gather | solution.py:174
  122.4 0.1 compare_reduce_fusion
  122.5 0.2 fusion.20
  122.7 0.1 iota_compare_fusion
  122.8 0.8 broadcast_and_fusion
  123.7 47.1 %all-gather.6.cloned.1.call-done = bf16[512,2880]{0,1:T(8,128)(2,1)} async-done(((bf16[128,2880]{0,1:T(8,128)(2,1)}), bf16[512,2880]{0,1:T(8,128)(2,1)}) %all-gather.6.cloned.1.call-update) | async-done | bytes 2949136 | tf_op jit(solution)/shard_map/all_gather | solution.py:205
  170.8 8.7 %convolution_convert_fusion.1 = bf16[1280,2880]{0,1:T(8,128)(2,1)} fusion(bf16[512,2880]{0,1:T(8,128)(2,1)} %all-gather.6.cloned.1.call-done, pred[160,8,4,128]{3,2,1,0:T(4,128)(4,1)S(1)} %bitcast.91), kind=kOutput, calls=%fused_computation.1 | convolution fusion | flops 3778560000 | bytes 10977280 | tf_op jit(solution)/shard_map/dot_general | solution.py:213
  179.6 10.4 %copy.61 = bf16[1280,2880]{1,0:T(8,128)(2,1)} copy(bf16[1280,2880]{0,1:T(8,128)(2,1)} %convolution_convert_fusion.1) | data formatting | bytes 14745600 | tf_op jit(solution)/shard_map/convert_element_type | solution.py:217
  190.0 88.9 %all_to_all.21 = bf16[8,160,2880]{2,1,0:T(8,128)(2,1)S(1)} all-to-all(bf16[8,160,2880]{2,1,0:T(8,128)(2,1)} %bitcast.80), channel_id=1, replica_groups=mesh['ctx'=8,'grp'=4] {'ctx'}, dimensions={0} | all-to-all | bytes 14745600 | tf_op jit(solution)/shard_map/all_to_all | solution.py:219
  278.9 15.3 %fusion = f32[1280,1536]{1,0:T(8,128)S(1)} fusion(bf16[1280,2880]{1,0:T(8,128)(2,1)S(1)} %bitcast.81, bf16[1,2880,1536]{2,1,0:T(8,128)(2,1)} %param.22), kind=kOutput, calls=%fused_computation.2 | convolution fusion | flops 11324620800 | bytes 24084480 | tf_op jit(solution)/shard_map/dot_general | solution.py:222
  294.3 8.3 %convolution_convert_fusion = bf16[1280,2880]{0,1:T(8,128)(2,1)} fusion(bf16[1,768,2880]{1,2,0:T(8,128)(2,1)S(1)} %bitcast.96, f32[1280,1536]{1,0:T(8,128)S(1)} %fusion), kind=kOutput, calls=%fused_computation | convolution fusion | flops 5673861120 | bytes 19660800 | tf_op jit(solution)/shard_map/dot_general | solution.py:224
  302.6 10.5 %copy.62 = bf16[1280,2880]{1,0:T(8,128)(2,1)} copy(bf16[1280,2880]{0,1:T(8,128)(2,1)} %convolution_convert_fusion) | data formatting | bytes 14745600 | tf_op jit(solution)/shard_map/convert_element_type | solution.py:224
  313.0 5.1 %all-to-all-start.3 = ((bf16[8,160,2880]{2,1,0:T(8,128)(2,1)}), bf16[8,160,2880]{2,1,0:T(8,128)(2,1)}, u32[]{:S(2)}, u32[]{:S(2)}) async-start(bf16[8,160,2880]{2,1,0:T(8,128)(2,1)} %bitcast.79), calls=%async_computation.3 | async-start | bytes 15073280 | tf_op jit(solution)/shard_map/all_to_all | solution.py:227
  318.2 0.3 reduce-scatter.2.cloned.1.call-start
  318.5 0.5 fusion.7
  319.0 0.1 fusion.23
  319.1 0.1 select_convert_fusion
  319.2 0.7 broadcast_select_fusion
  319.9 0.2 copy.80
  320.2 0.6 copy.66
  320.8 82.3 %all-to-all-done.3 = bf16[8,160,2880]{2,1,0:T(8,128)(2,1)} async-done(((bf16[8,160,2880]{2,1,0:T(8,128)(2,1)}), bf16[8,160,2880]{2,1,0:T(8,128)(2,1)}, u32[]{:S(2)}, u32[]{:S(2)}) %all-to-all-start.3) | async-done | bytes 7372832 | tf_op jit(solution)/shard_map/all_to_all | solution.py:227
  403.1 7.8 %convolution_convert_fusion.2 = bf16[4,128,2880]{1,2,0:T(8,128)(2,1)} fusion(bf16[4,128,1280]{2,1,0:T(8,128)(2,1)S(1)} %bitcast.89, bf16[1280,2880,1]{1,0,2:T(8,128)(2,1)} %bitcast.27), kind=kOutput, calls=%fused_computation.4 | convolution fusion | flops 3776348160 | bytes 11632640 | tf_op jit(solution)/shard_map/dot_general | solution.py:233
  410.9 53.8 %reduce-scatter.2.cloned.1.call-done = bf16[1,128,2880]{1,2,0:T(8,128)(2,1)} async-done(((bf16[4,128,2880]{1,2,0:T(8,128)(2,1)}), bf16[1,128,2880]{1,2,0:T(8,128)(2,1)}) %reduce-scatter.2.cloned.1.call-update) | async-done | bytes 737296 | tf_op jit(solution)/shard_map/reduce_scatter | solution.py:239
  464.7 2.2 fusion.21
  (36 shorter events, 0.2 us)
Async XLA Ops:
  7.2 311.3 %copy-start = (bf16[2880,16]{0,1:T(8,128)(2,1)S(1)}, bf16[2880,16]{0,1:T(8,128)(2,1)}, u32[]{:S(2)}) copy-start(bf16[2880,16]{0,1:T(8,128)(2,1)} %param.20) | copy-start | bytes 276484
  7.2 3.4 copy-start.4
  7.2 93.3 %all-gather.4.cloned.1.call-start = ((), (), s32[]{:S(2)}) async-start(), calls=%async_computation.5 | async-start | bytes 13271040 | tf_op jit(solution)/shard_map/all_gather | solution.py:173
  11.4 6.5 %copy-start.8 = (s32[1,8]{1,0:T(1,128)S(1)}, s32[1,8]{1,0:T(1,128)}, u32[]{:S(2)}) copy-start(s32[1,8]{1,0:T(1,128)} %param.16) | copy-start | bytes 100
  11.4 6.6 %copy-start.9 = (f32[32]{0:T(128)S(1)}, f32[32]{0:T(128)}, u32[]{:S(2)}) copy-start(f32[32]{0:T(128)} %param.17) | copy-start | bytes 388
  12.6 35.0 %all-to-all-start = ((bf16[8,640,128]{2,1,0:T(8,128)(2,1)}), bf16[8,640,128]{2,1,0:T(8,128)(2,1)S(1)}, u32[]{:S(2)}, u32[]{:S(2)}) async-start(bf16[8,640,128]{2,1,0:T(8,128)(2,1)} %pad_maximum_fusion), calls=%async_computation | async-start | bytes 2621440 | tf_op jit(solution)/shard_map/all_to_all | solution.py:123
  17.8 153.0 %all-gather.6.cloned.1.call-start = ((), (), s32[]{:S(2)}) async-start(), calls=%async_computation.7 | async-start | bytes 3686400 | tf_op jit(solution)/shard_map/all_gather | solution.py:205
  47.7 52.8 %copy-start.7 = (bf16[1,128,2880]{1,2,0:T(8,128)(2,1)S(1)}, bf16[1,128,2880]{1,2,0:T(8,128)(2,1)}, u32[]{:S(2)}) copy-start(bf16[1,128,2880]{1,2,0:T(8,128)(2,1)} %param.12) | copy-start | bytes 2211844
  100.5 8.5 %copy-start.5 = (f32[2880]{0:T(1024)S(1)}, f32[2880]{0:T(1024)}, u32[]{:S(2)}) copy-start(f32[2880]{0:T(1024)} %param.19) | copy-start | bytes 34564
  100.5 9.9 %copy-start.6 = (s32[1,128,4]{1,2,0:T(4,128)S(1)}, s32[1,128,4]{1,2,0:T(4,128)}, u32[]{:S(2)}) copy-start(s32[1,128,4]{1,2,0:T(4,128)} %param.21) | copy-start | bytes 6148
  108.2 0.9 copy-start.2
  190.0 104.2 %slice-start = ((s8[4423680]{0:T(1024)(128)(4,1)}), s8[4194304]{0:T(1024)(128)(4,1)S(1)}, s32[]{:S(2)}) async-start(s8[4423680]{0:T(1024)(128)(4,1)} %bitcast.95), calls=%async_computation.8 | async-start | bytes 8388608
  278.9 15.3 %slice-start.1 = ((s8[4423680]{0:T(1024)(128)(4,1)}), s8[229376]{0:T(1024)(128)(4,1)S(1)}, s32[]{:S(2)}) async-start(s8[4423680]{0:T(1024)(128)(4,1)} %bitcast.95), calls=%async_computation.9 | async-start | bytes 458752
  313.0 5.4 %copy-start.1 = (bf16[512,2880]{0,1:T(8,128)(2,1)S(1)}, bf16[512,2880]{0,1:T(8,128)(2,1)}, u32[]{:S(2)}) copy-start(bf16[512,2880]{0,1:T(8,128)(2,1)} %all-gather.6.cloned.1.call-done) | copy-start | bytes 8847364
  313.0 90.1 %all-to-all-start.3 = ((bf16[8,160,2880]{2,1,0:T(8,128)(2,1)}), bf16[8,160,2880]{2,1,0:T(8,128)(2,1)}, u32[]{:S(2)}, u32[]{:S(2)}) async-start(bf16[8,160,2880]{2,1,0:T(8,128)(2,1)} %bitcast.79), calls=%async_computation.3 | async-start | bytes 15073280 | tf_op jit(solution)/shard_map/all_to_all | solution.py:227
  318.2 146.5 %reduce-scatter.2.cloned.1.call-start = ((), (), s32[]{:S(2)}) async-start(), calls=%async_computation.6 | async-start | bytes 3686400 | tf_op jit(solution)/shard_map/reduce_scatter | solution.py:239
  410.9 53.8 %copy-start.3 = (bf16[128,2880]{0,1:T(8,128)(2,1)S(1)}, bf16[128,2880]{0,1:T(8,128)(2,1)}, u32[]{:S(2)}) copy-start(bf16[128,2880]{0,1:T(8,128)(2,1)} %copy-done.2) | copy-start | bytes 2211844
Sparse Core Ops, SparseCore 0:
  9.9 90.5 all-gather.3
  110.5 60.2 all-gather.5
  411.0 53.6 reduce-scatter.1

commit v3 on v2

--- a/solution.py
+++ b/solution.py
@@ -202,7 +202,9 @@
         * lax.rsqrt(jnp.mean(mid_float * mid_float, axis=-1, keepdims=True) + 1e-05)
         * norm_gain
     ).astype(jnp.bfloat16)
-    column = lax.all_gather(normed, "grp", axis=0)
+    cuts = ((0, width // 256 * 128 + 128), (width // 256 * 128 + 128, width))
+    columns = [lax.all_gather(normed[:, lo:hi], "grp", axis=0) for lo, hi in cuts]
+    column = jnp.concatenate(columns, axis=2)
     logits = jnp.einsum("gtd,de->gte", column, router, preferred_element_type=jnp.float32)
     picks = ids_all[..., None] == jnp.arange(experts, dtype=jnp.int32)
     chosen = jnp.sum(jnp.where(picks, logits[:, :, None, :], 0.0), axis=-1)
@@ -210,33 +212,40 @@
     route_weights = raised / jnp.sum(raised, axis=-1, keepdims=True)
     by_expert = jnp.sum(jnp.where(named, route_weights[..., None], 0.0), axis=2)
 
-    packed = jnp.dot(
-        spread.astype(jnp.bfloat16),
-        column.reshape(-1, width),
-        preferred_element_type=jnp.float32,
-    ).astype(jnp.bfloat16)
-    packed = packed.reshape(ctx_count, grp_count * capacity, width)
-    received = lax.all_to_all(packed, "ctx", split_axis=0, concat_axis=0, tiled=True)
+    packing = spread.astype(jnp.bfloat16)
+
+    def exchange(rows):
+        blocks = rows.astype(jnp.bfloat16).reshape(ctx_count, grp_count * capacity, -1)
+        moved = lax.all_to_all(blocks, "ctx", split_axis=0, concat_axis=0, tiled=True)
+        return moved.reshape(rows.shape)
+
+    received = [
+        exchange(
+            jnp.dot(packing, c.reshape(-1, c.shape[2]), preferred_element_type=jnp.float32)
+        )
+        for c in columns
+    ]
     in_weights = expert_in[0]
     out_weights = expert_out[0]
-    pre = jnp.dot(received.reshape(-1, width), in_weights, preferred_element_type=jnp.float32)
+    pre = sum(
+        jnp.dot(r, in_weights[lo:hi], preferred_element_type=jnp.float32)
+        for r, (lo, hi) in zip(received, cuts)
+    )
     hidden = gated_act(pre, out_weights.shape[0])
-    partial_out = jnp.dot(hidden, out_weights, preferred_element_type=jnp.float32).astype(
-        jnp.bfloat16
-    )
-    returned = lax.all_to_all(
-        partial_out.reshape(received.shape), "ctx", split_axis=0, concat_axis=0, tiled=True
-    )
+    returned = [
+        exchange(jnp.dot(hidden, out_weights[:, lo:hi], preferred_element_type=jnp.float32))
+        for lo, hi in cuts
+    ]
     scale = jnp.transpose(by_expert, (2, 0, 1))[:, :, None, :]
     weighted = jnp.where(places, scale, 0.0).astype(jnp.bfloat16)[:, :, :, None, :]
     weighted = jnp.where(same, weighted, jnp.zeros_like(weighted)).reshape(spread.shape)
-    mixture = lax.dot_general(
-        weighted,
-        returned.reshape(-1, width),
-        (((0,), (0,)), ((), ())),
-        preferred_element_type=jnp.float32,
-    ).reshape(grp_count, tokens, width)
-    sums = lax.psum_scatter(mixture.astype(jnp.bfloat16), "grp", scatter_dimension=0)
+    sums = []
+    for part in returned:
+        mixture = lax.dot_general(
+            weighted, part, (((0,), (0,)), ((), ())), preferred_element_type=jnp.float32
+        ).reshape(grp_count, tokens, -1)
+        sums.append(lax.psum_scatter(mixture.astype(jnp.bfloat16), "grp", scatter_dimension=0))
+    sums = jnp.concatenate(sums, axis=1)
     final = (mid_float + sums.astype(jnp.float32)).astype(jnp.bfloat16)
     return (mid[None], final[None])
 

time: 474 us -> 419 us (0.88)
  blocking collectives: 119 us -> 30.1 us
  waiting for transfers between devices: 217 us -> 235 us
  matrix products: 48.5 us -> 62.2 us
  starting transfers between devices: 10.6 us -> 24.2 us
  local copies, waits for them, and re-layouts: 26.6 us -> 17.7 us
    all_to_all x1 -> x0, blocking collectives: 88.9 us -> none  [body(): lax.all_to_all(packed, 'ctx', split_axis=0, concat_axis=0, tiled=True)]
    all_to_all x1 -> x4, waiting for transfers between devices: 82.3 us -> 105 us  [exchange(): lax.all_to_all(blocks, 'ctx', split_axis=0, concat_axis=0, tiled=True)]
    reduce_scatter x1 -> x2, waiting for transfers between devices: 53.8 us -> 33 us  [body(): lax.psum_scatter(mixture.astype(jnp.bfloat16), 'grp', scatter_dimension=0)]
    convert_element_type x2, local copies, waits for them, and re-layouts: 20.9 us -> 7.17 us  [exchange(): rows.astype(jnp.bfloat16).reshape(ctx_count, grp_count * capacity, -1)]
    dot_general x4 -> x8, matrix products: 40.1 us -> 53.8 us  [the longest x2 21.6 us: body(): jnp.dot(r, in_weights[lo:hi], preferred_element_type=jnp.float32)]
    all_to_all x1 -> x4, starting transfers between devices: 5.13 us -> 18.6 us  [exchange(): lax.all_to_all(blocks, 'ctx', split_axis=0, concat_axis=0, tiled=True)]
    all_gather x1 -> x2, waiting for transfers between devices: 47.1 us -> 60 us  [body(): lax.all_gather(normed[:, lo:hi], 'grp', axis=0)]
  transfers between devices with their start and end apart: 5 -> 10, of which waited for: 5 -> 9; matrix products, arithmetic and copies ran while one was open for 2% -> 11% of each run, Pallas kernels for 6% -> 7%
where the time goes in v3:
time: 419 us; the launch traced here: 418 us
  waiting for transfers between devices  235 us (56%)
  matrix products  62.2 us (15%)
  blocking collectives  30.1 us (7%)
  Pallas kernels  27.7 us (7%)
  starting transfers between devices  24.2 us (6%)
  local copies, waits for them, and re-layouts  17.7 us (4%)
  between operations  14.2 us (3%)
  other arithmetic  7.29 us (2%)
    all_to_all x4, waiting for transfers between devices, exchange(): lax.all_to_all(blocks, 'ctx', split_axis=0, concat_axis=0, tiled=True)  105 us
    all_gather x2, waiting for transfers between devices, body(): lax.all_gather(normed[:, lo:hi], 'grp', axis=0)  60 us
    reduce_scatter x2, waiting for transfers between devices, body(): lax.psum_scatter(mixture.astype(jnp.bfloat16), 'grp', scatter_dimension=0)  33 us
    all_to_all x1, waiting for transfers between devices, attention(): recv = lax.all_to_all(sent, 'ctx', split_axis=0, concat_axis=0, tiled=True)  28.4 us
    pallas_call x1, Pallas kernels, attention(): pl.pallas_call(functools.partial(attention_kernel, cache_rows, tokens), o...  27.7 us
    dot_general x2, matrix products, body(): jnp.dot(r, in_weights[lo:hi], preferred_element_type=jnp.float32)  21.6 us
    all_to_all x4, starting transfers between devices, exchange(): lax.all_to_all(blocks, 'ctx', split_axis=0, concat_axis=0, tiled=True)  18.6 us
    all_to_all x1, blocking collectives, attention(): lax.all_to_all(attended, 'ctx', split_axis=0, concat_axis=0, tiled=True)  18.1 us
  transfers between devices with their start and end apart: 10, of which 9 were waited for; matrix products, arithmetic and copies ran while one was open for 11% of the time, Pallas kernels for 7%

profile of v3, /device:TPU:0, one launch (start us, length us, event | category | flops | bytes accessed | tf_op | source)
XLA Modules:
  0.0 418.4 jit_solution(12176453839688532909)
XLA Ops:
  7.2 0.7 all-gather.6.cloned.1.call-update
  7.9 1.4 reshape_squeeze.3
  10.1 0.4 copy.64
  10.5 1.2 pad_maximum_fusion
  11.7 5.2 %all-to-all-start = ((bf16[8,640,128]{2,1,0:T(8,128)(2,1)}), bf16[8,640,128]{2,1,0:T(8,128)(2,1)S(1)}, u32[]{:S(2)}, u32[]{:S(2)}) async-start(bf16[8,640,128]{2,1,0:T(8,128)(2,1)} %pad_maximum_fusion), calls=%async_computation | async-start | bytes 2621440 | tf_op jit(solution)/shard_map/all_to_all | solution.py:123
  17.5 28.4 %all-to-all-done.recv_ref = bf16[8,640,128]{2,1,0:T(8,128)(2,1)S(1)} async-done(((bf16[8,640,128]{2,1,0:T(8,128)(2,1)}), bf16[8,640,128]{2,1,0:T(8,128)(2,1)S(1)}, u32[]{:S(2)}, u32[]{:S(2)}) %all-to-all-start) | async-done | bytes 1310752 | tf_op jit(solution)/shard_map/all_to_all | solution.py:123
  46.0 27.7 %shard_map.131 = bf16[8,128,256]{2,1,0:T(8,128)(2,1)S(1)} custom-call(s32[8]{0:T(128)S(1)} %slice_reduce_fusion.lows, bf16[8,640,128]{2,1,0:T(8,128)(2,1)S(1)} %all-to-all-done.recv_ref, s32[8,1,128]{2,1,0:T(1,128)S(1)} %bitcast.94, f32[1,512]{1,0:T(1,128)S(1)} %bitcast.95), custom_call_target="tpu_custom_call" | custom-call | flops 8000000000 | bytes 2000000 | tf_op jit(solution)/shard_map/pallas_call | solution.py:131
  73.7 18.1 %all_to_all.30 = bf16[8,128,256]{2,1,0:T(8,128)(2,1)S(1)} all-to-all(bf16[8,128,256]{2,1,0:T(8,128)(2,1)S(1)} %shard_map.131), channel_id=1, replica_groups=mesh['ctx'=8,'grp'=4] {'ctx'}, dimensions={0} | all-to-all | bytes 1048576 | tf_op jit(solution)/shard_map/all_to_all | solution.py:147
  91.8 0.3 copy.65
  92.1 7.6 %all-gather.6.cloned.1.call-done = bf16[2048,2880]{0,1:T(8,128)(2,1)} async-done(((bf16[256,2880]{0,1:T(8,128)(2,1)}), bf16[2048,2880]{0,1:T(8,128)(2,1)}) %all-gather.6.cloned.1.call-update) | async-done | bytes 11796496 | tf_op jit(solution)/shard_map/all_gather | solution.py:173
  99.7 7.6 %fusion.19 = (f32[128]{0:T(128)S(1)}, bf16[128,2880]{0,1:T(8,128)(2,1)S(1)}) fusion(bf16[2048,2880]{0,1:T(8,128)(2,1)} %all-gather.6.cloned.1.call-done, bf16[128,2048]{0,1:T(8,128)(2,1)S(1)} %bitcast.112, bf16[1,128,2880]{1,2,0:T(8,128)(2,1)S(1)} %copy-done.16), kind=kOutput, calls=%fused_computation.32 | convolution fusion | flops 1512161152 | bytes 13795840 | tf_op jit(solution)/shard_map/dot_general | solution.py:197
  107.3 0.8 copy-done.1
  108.2 0.4 fusion.21
  108.6 0.8 slice.45
  109.4 12.0 %all_gather.19 = s32[4,128,4]{1,2,0:T(4,128)S(1)} all-gather(s32[1,128,4]{1,2,0:T(4,128)S(1)} %copy-done.13), channel_id=1, replica_groups=mesh['ctx'=8,'grp'=4] {'grp'}, dimensions={0}, use_global_device_ids=true | all-gather | bytes 10240 | tf_op jit(solution)/shard_map/all_gather | solution.py:174
  121.8 0.2 copy-done.10
  122.1 0.8 broadcast_and_fusion
  123.0 24.3 %all-gather.8.cloned.1.call-done = bf16[512,1536]{0,1:T(8,128)(2,1)} async-done(((bf16[128,1536]{0,1:T(8,128)(2,1)}), bf16[512,1536]{0,1:T(8,128)(2,1)}) %all-gather.8.cloned.1.call-update) | async-done | bytes 1572880 | tf_op jit(solution)/shard_map/all_gather | solution.py:206
  147.3 5.5 %convolution_convert_fusion.3 = bf16[1280,1536]{1,0:T(8,128)(2,1)} fusion(bf16[512,1536]{0,1:T(8,128)(2,1)} %all-gather.8.cloned.1.call-done, pred[160,8,4,128]{3,2,1,0:T(4,128)(4,1)S(1)} %bitcast.110), kind=kOutput, calls=%fused_computation.4 | convolution fusion | flops 2015232000 | bytes 6160384 | tf_op jit(solution)/shard_map/dot_general | solution.py:224
  152.8 4.6 %all-to-all-start.2 = ((bf16[8,160,1536]{2,1,0:T(8,128)(2,1)}), bf16[8,160,1536]{2,1,0:T(8,128)(2,1)}, u32[]{:S(2)}, u32[]{:S(2)}) async-start(bf16[8,160,1536]{2,1,0:T(8,128)(2,1)} %bitcast.101), calls=%async_computation.2 | async-start | bytes 7864320 | tf_op jit(solution)/shard_map/all_to_all | solution.py:219
  157.6 0.8 slice.46
  158.4 35.7 %all-gather.10.cloned.1.call-done = bf16[512,1344]{0,1:T(8,128)(2,1)} async-done(((bf16[128,1344]{0,1:T(8,128)(2,1)}), bf16[512,1344]{0,1:T(8,128)(2,1)}) %all-gather.10.cloned.1.call-update) | async-done | bytes 1376272 | tf_op jit(solution)/shard_map/all_gather | solution.py:206
  194.1 3.5 convolution_convert_fusion.2
  197.6 3.5 copy.70
  201.2 2.5 all-to-all-done.2
  203.7 4.5 %all-to-all-start.3 = ((bf16[8,160,1344]{2,1,0:T(8,128)(2,1)}), bf16[8,160,1344]{2,1,0:T(8,128)(2,1)}, u32[]{:S(2)}, u32[]{:S(2)}) async-start(bf16[8,160,1344]{2,1,0:T(8,128)(2,1)} %bitcast.97), calls=%async_computation.3 | async-start | bytes 7208960 | tf_op jit(solution)/shard_map/all_to_all | solution.py:219
  208.2 11.3 %fusion = f32[1280,1536]{1,0:T(8,128)} fusion(bf16[1280,1536]{1,0:T(8,128)(2,1)} %bitcast.21, bf16[1,2880,1536]{2,1,0:T(8,128)(2,1)} %param.22), kind=kOutput, calls=%fused_computation.5 | convolution fusion | flops 6039797760 | bytes 16515072 | tf_op jit(solution)/shard_map/dot_general | solution.py:231
  219.5 31.5 %all-to-all-done.3 = bf16[8,160,1344]{2,1,0:T(8,128)(2,1)} async-done(((bf16[8,160,1344]{2,1,0:T(8,128)(2,1)}), bf16[8,160,1344]{2,1,0:T(8,128)(2,1)}, u32[]{:S(2)}, u32[]{:S(2)}) %all-to-all-start.3) | async-done | bytes 3440672 | tf_op jit(solution)/shard_map/all_to_all | solution.py:219
  251.0 10.3 %convolution_add_fusion = f32[1280,1536]{1,0:T(8,128)S(1)} fusion(f32[1280,1536]{1,0:T(8,128)} %fusion, bf16[1280,1344]{1,0:T(8,128)(2,1)} %bitcast.24, bf16[1,2880,1536]{2,1,0:T(8,128)(2,1)} %param.22), kind=kOutput, calls=%fused_computation | convolution fusion | flops 5286789120 | bytes 23461888 | tf_op jit(solution)/shard_map/dot_general | solution.py:231
  261.3 1.1 fusion.7
  262.4 1.3 copy-done.3
  263.7 4.5 %convolution_convert_fusion = bf16[1280,1344]{0,1:T(8,128)(2,1)S(1)} fusion(bf16[1280,768]{1,0:T(8,128)(2,1)S(1)} %fusion.7, bf16[768,2880]{0,1:T(8,128)(2,1)} %bitcast.117), kind=kOutput, calls=%fused_computation.1 | convolution fusion | flops 2644131840 | bytes 7471104 | tf_op jit(solution)/shard_map/dot_general | solution.py:236
  268.2 3.6 copy.73
  271.8 4.9 %all-to-all-start.5 = ((bf16[8,160,1344]{2,1,0:T(8,128)(2,1)}), bf16[8,160,1344]{2,1,0:T(8,128)(2,1)}, u32[]{:S(2)}, u32[]{:S(2)}) async-start(bf16[8,160,1344]{2,1,0:T(8,128)(2,1)} %bitcast.96), calls=%async_computation.6 | async-start | bytes 7208960 | tf_op jit(solution)/shard_map/all_to_all | solution.py:219
  277.0 1.2 copy-done.5
  278.1 0.3 copy_bitcast_fusion
  278.4 0.5 fusion.9
  279.2 0.8 copy-done.4
  280.0 6.4 %convolution_convert_fusion.1 = bf16[1280,1536]{1,0:T(8,128)(2,1)} fusion(bf16[1280,768]{1,0:T(8,128)(2,1)S(1)} %copy-done.4, bf16[768,2880]{0,1:T(8,128)(2,1)} %bitcast.118), kind=kOutput, calls=%fused_computation.2 | convolution fusion | flops 3021864960 | bytes 8257536 | tf_op jit(solution)/shard_map/dot_general | solution.py:236
  286.4 32.9 %all-to-all-done.5 = bf16[8,160,1344]{2,1,0:T(8,128)(2,1)} async-done(((bf16[8,160,1344]{2,1,0:T(8,128)(2,1)}), bf16[8,160,1344]{2,1,0:T(8,128)(2,1)}, u32[]{:S(2)}, u32[]{:S(2)}) %all-to-all-start.5) | async-done | bytes 3440672 | tf_op jit(solution)/shard_map/all_to_all | solution.py:219
  319.3 4.7 %all-to-all-start.4 = ((bf16[8,160,1536]{2,1,0:T(8,128)(2,1)}), bf16[8,160,1536]{2,1,0:T(8,128)(2,1)}, u32[]{:S(2)}, u32[]{:S(2)}) async-start(bf16[8,160,1536]{2,1,0:T(8,128)(2,1)} %bitcast.100), calls=%async_computation.4 | async-start | bytes 7864320 | tf_op jit(solution)/shard_map/all_to_all | solution.py:219
  324.3 0.7 broadcast_select_fusion
  325.2 0.6 copy.79
  325.8 5.9 %convolution_convert_fusion.4 = bf16[4,128,1344]{1,2,0:T(8,128)(2,1)} fusion(bf16[4,128,1280]{2,1,0:T(8,128)(2,1)S(1)} %bitcast.107, bf16[1280,1344,1]{1,0,2:T(8,128)(2,1)} %bitcast.33), kind=kOutput, calls=%fused_computation.16 | convolution fusion | flops 1762295808 | bytes 6127616 | tf_op jit(solution)/shard_map/dot_general | solution.py:244
  331.8 38.5 %all-to-all-done.4 = bf16[8,160,1536]{2,1,0:T(8,128)(2,1)} async-done(((bf16[8,160,1536]{2,1,0:T(8,128)(2,1)}), bf16[8,160,1536]{2,1,0:T(8,128)(2,1)}, u32[]{:S(2)}, u32[]{:S(2)}) %all-to-all-start.4) | async-done | bytes 3932192 | tf_op jit(solution)/shard_map/all_to_all | solution.py:219
  370.3 6.4 %convolution_convert_fusion.5 = bf16[4,128,1536]{1,2,0:T(8,128)(2,1)} fusion(bf16[4,128,1280]{2,1,0:T(8,128)(2,1)S(1)} %bitcast.108, bf16[1280,1536,1]{1,0,2:T(8,128)(2,1)} %bitcast.29), kind=kOutput, calls=%fused_computation.17 | convolution fusion | flops 2014052352 | bytes 6815744 | tf_op jit(solution)/shard_map/dot_general | solution.py:244
  376.7 33.0 %reduce-scatter.3.cloned.1.call-done = bf16[1,128,1536]{1,2,0:T(8,128)(2,1)} async-done(((bf16[4,128,1536]{1,2,0:T(8,128)(2,1)}), bf16[1,128,1536]{1,2,0:T(8,128)(2,1)}) %reduce-scatter.3.cloned.1.call-update) | async-done | bytes 393232 | tf_op jit(solution)/shard_map/reduce_scatter | solution.py:247
  409.7 2.2 fusion.25
  (69 shorter events, 3.2 us)
Async XLA Ops:
  7.2 271.2 %copy-start = (bf16[2880,16]{0,1:T(8,128)(2,1)S(1)}, bf16[2880,16]{0,1:T(8,128)(2,1)}, u32[]{:S(2)}) copy-start(bf16[2880,16]{0,1:T(8,128)(2,1)} %param.20) | copy-start | bytes 276484
  7.2 2.3 copy-start.9
  7.2 2.5 copy-start.8
  7.2 92.4 %all-gather.6.cloned.1.call-start = ((), (), s32[]{:S(2)}) async-start(), calls=%async_computation.8 | async-start | bytes 13271040 | tf_op jit(solution)/shard_map/all_gather | solution.py:173
  10.5 6.5 %copy-start.17 = (s32[1,8]{1,0:T(1,128)S(1)}, s32[1,8]{1,0:T(1,128)}, u32[]{:S(2)}) copy-start(s32[1,8]{1,0:T(1,128)} %param.16) | copy-start | bytes 100
  10.5 6.6 %copy-start.18 = (f32[32]{0:T(128)S(1)}, f32[32]{0:T(128)}, u32[]{:S(2)}) copy-start(f32[32]{0:T(128)} %param.17) | copy-start | bytes 388
  11.7 34.2 %all-to-all-start = ((bf16[8,640,128]{2,1,0:T(8,128)(2,1)}), bf16[8,640,128]{2,1,0:T(8,128)(2,1)S(1)}, u32[]{:S(2)}, u32[]{:S(2)}) async-start(bf16[8,640,128]{2,1,0:T(8,128)(2,1)} %pad_maximum_fusion), calls=%async_computation | async-start | bytes 2621440 | tf_op jit(solution)/shard_map/all_to_all | solution.py:123
  16.9 130.4 %all-gather.8.cloned.1.call-start = ((), (), s32[]{:S(2)}) async-start(), calls=%async_computation.11 | async-start | bytes 1966080 | tf_op jit(solution)/shard_map/all_gather | solution.py:206
  46.0 53.7 %copy-start.16 = (bf16[1,128,2880]{1,2,0:T(8,128)(2,1)S(1)}, bf16[1,128,2880]{1,2,0:T(8,128)(2,1)}, u32[]{:S(2)}) copy-start(bf16[1,128,2880]{1,2,0:T(8,128)(2,1)} %param.12) | copy-start | bytes 2211844
  99.7 8.5 %copy-start.12 = (f32[2880]{0:T(1024)S(1)}, f32[2880]{0:T(1024)}, u32[]{:S(2)}) copy-start(f32[2880]{0:T(1024)} %param.19) | copy-start | bytes 34564
  107.3 0.9 copy-start.1
  107.3 2.1 copy-start.13
  121.4 0.6 copy-start.10
  122.0 30.8 %copy-start.14 = (pred[4,4]{1,0:T(4,128)(4,1)}, pred[4,4]{1,0:T(4,128)(4,1)S(1)}, u32[]{:S(2)}) copy-start(pred[4,4]{1,0:T(4,128)(4,1)S(1)} %iota_compare_fusion.3) | copy-start | bytes 52
  123.0 29.8 %copy-start.7 = (pred[8,4,40,4,128]{4,3,2,1,0:T(4,128)(4,1)}, pred[8,4,40,4,128]{4,3,2,1,0:T(4,128)(4,1)S(1)}, u32[]{:S(2)}) copy-start(pred[8,4,40,4,128]{4,3,2,1,0:T(4,128)(4,1)S(1)} %broadcast_and_fusion) | copy-start | bytes 1966084
  152.8 50.9 %all-to-all-start.2 = ((bf16[8,160,1536]{2,1,0:T(8,128)(2,1)}), bf16[8,160,1536]{2,1,0:T(8,128)(2,1)}, u32[]{:S(2)}, u32[]{:S(2)}) async-start(bf16[8,160,1536]{2,1,0:T(8,128)(2,1)} %bitcast.101), calls=%async_computation.2 | async-start | bytes 7864320 | tf_op jit(solution)/shard_map/all_to_all | solution.py:219
  157.4 36.7 %all-gather.10.cloned.1.call-start = ((), (), s32[]{:S(2)}) async-start(), calls=%async_computation.12 | async-start | bytes 1720320 | tf_op jit(solution)/shard_map/all_gather | solution.py:206
  203.7 47.3 %all-to-all-start.3 = ((bf16[8,160,1344]{2,1,0:T(8,128)(2,1)}), bf16[8,160,1344]{2,1,0:T(8,128)(2,1)}, u32[]{:S(2)}, u32[]{:S(2)}) async-start(bf16[8,160,1344]{2,1,0:T(8,128)(2,1)} %bitcast.97), calls=%async_computation.3 | async-start | bytes 7208960 | tf_op jit(solution)/shard_map/all_to_all | solution.py:219
  262.4 1.3 copy-start.3
  271.8 4.9 %copy-start.6 = (bf16[512,1344]{0,1:T(8,128)(2,1)S(1)}, bf16[512,1344]{0,1:T(8,128)(2,1)}, u32[]{:S(2)}) copy-start(bf16[512,1344]{0,1:T(8,128)(2,1)} %all-gather.10.cloned.1.call-done) | copy-start | bytes 4128772
  271.8 47.5 %all-to-all-start.5 = ((bf16[8,160,1344]{2,1,0:T(8,128)(2,1)}), bf16[8,160,1344]{2,1,0:T(8,128)(2,1)}, u32[]{:S(2)}, u32[]{:S(2)}) async-start(bf16[8,160,1344]{2,1,0:T(8,128)(2,1)} %bitcast.96), calls=%async_computation.6 | async-start | bytes 7208960 | tf_op jit(solution)/shard_map/all_to_all | solution.py:219
  276.7 1.4 copy-start.5
  278.4 0.7 copy-start.11
  278.4 1.6 copy-start.4
  319.3 4.9 %copy-start.15 = (pred[4,4]{1,0:T(4,128)(4,1)S(1)}, pred[4,4]{1,0:T(4,128)(4,1)}, u32[]{:S(2)}) copy-start(pred[4,4]{1,0:T(4,128)(4,1)} %copy-done.14) | copy-start | bytes 52
  319.3 51.0 %all-to-all-start.4 = ((bf16[8,160,1536]{2,1,0:T(8,128)(2,1)}), bf16[8,160,1536]{2,1,0:T(8,128)(2,1)}, u32[]{:S(2)}, u32[]{:S(2)}) async-start(bf16[8,160,1536]{2,1,0:T(8,128)(2,1)} %bitcast.100), calls=%async_computation.4 | async-start | bytes 7864320 | tf_op jit(solution)/shard_map/all_to_all | solution.py:219
  324.0 52.8 %reduce-scatter.5.cloned.1.call-start = ((), (), s32[]{:S(2)}) async-start(), calls=%async_computation.10 | async-start | bytes 1720320 | tf_op jit(solution)/shard_map/reduce_scatter | solution.py:247
  331.8 78.0 %reduce-scatter.3.cloned.1.call-start = ((), (), s32[]{:S(2)}) async-start(), calls=%async_computation.9 | async-start | bytes 1966080 | tf_op jit(solution)/shard_map/reduce_scatter | solution.py:247
  370.3 39.4 %copy-start.2 = (bf16[128,2880]{0,1:T(8,128)(2,1)S(1)}, bf16[128,2880]{0,1:T(8,128)(2,1)}, u32[]{:S(2)}) copy-start(bf16[128,2880]{0,1:T(8,128)(2,1)} %copy-done.1) | copy-start | bytes 2211844
Sparse Core Ops, SparseCore 0:
  9.9 89.6 all-gather.5
  109.5 37.7 all-gather.7
  159.8 34.2 all-gather.9
  331.9 31.9 reduce-scatter.4
  376.8 32.8 reduce-scatter.2
